TPU v7x, 32 devices: a whole 2x2x4 slice. The times are simulated.
32 devices in a mesh: shard: 8 (over z, x), ctx: 2 (over y), tensor: 2 (over core).
Axes of the slice: x: 2, y: 2, z: 4, core: 2. Of those that a mesh axis runs over, the one named last changes fastest.
Arguments:
- clip_input: bfloat16 [8, 8, 392, 512], P('shard', 'ctx', None, 'tensor'), may hold values from -6 to 6
- cotangent: bfloat16 [8, 8, 392, 512], P('shard', 'ctx', None, 'tensor'), may hold values from -6 to 6
- gain_one: float32 [512], P('tensor'), may hold values from 0.1 to 1.9
- shift_one: float32 [512], P('tensor'), may hold values from -3 to 3
- w_qkv: bfloat16 [3, 512, 512], P(None, 'shard', 'tensor'), may hold values from -0.25 to 0.25
- b_qv: float32 [2, 512], P(None, 'tensor'), may hold values from -3 to 3
- w_proj: bfloat16 [512, 512], P('tensor', 'shard'), may hold values from -1.5 to 1.5
- b_proj: float32 [512], P('tensor'), may hold values from -3 to 3
- bias_table: float32 [16, 2535], P('tensor'), may hold values from -3 to 3
- gain_two: float32 [512], P('tensor'), may hold values from 0.1 to 1.9
- shift_two: float32 [512], P('tensor'), may hold values from -3 to 3
- w_fc1: bfloat16 [512, 2048], P('shard', 'tensor'), may hold values from -0.25 to 0.25
- b_fc1: float32 [2048], P('tensor'), may hold values from -3 to 3
- w_fc2: bfloat16 [2048, 512], P('tensor', 'shard'), may hold values from -0.125 to 0.125
- b_fc2: float32 [512], P('tensor'), may hold values from -3 to 3
- rel_index: int32 [392, 392], replicated, may hold values from 0 to 2534
- regions: int32 [8, 392], P('ctx'), may hold values from 0 to 3
Outputs:
- block_out: float32 [8, 8, 392, 512], P('shard', 'ctx', None, 'tensor')
- grad_input: float32 [8, 8, 392, 512], P('shard', 'ctx', None, 'tensor')
- grad_gain_one: float32 [512], P('tensor')
- grad_shift_one: float32 [512], P('tensor')
- grad_w_qkv: float32 [3, 512, 512], P(None, 'shard', 'tensor')
- grad_b_qv: float32 [2, 512], P(None, 'tensor')
- grad_w_proj: float32 [512, 512], P('tensor', 'shard')
- grad_b_proj: float32 [512], P('tensor')
- grad_table: float32 [16, 2535], P('tensor')
- grad_gain_two: float32 [512], P('tensor')
- grad_shift_two: float32 [512], P('tensor')
- grad_w_fc1: float32 [512, 2048], P('shard', 'tensor')
- grad_b_fc1: float32 [2048], P('tensor')
- grad_w_fc2: float32 [2048, 512], P('tensor', 'shard')
- grad_b_fc2: float32 [512], P('tensor')
Inputs may be any that keep to these rules, and one draw needn't show every extreme that they name: `rel_index`: a table entry for every pair of a window's tokens.
All inputs are finite; a program needn't handle non-finite values.
Results may differ from a plain program's by a relative error of at most 0.015.
Values may be sent and summed in bfloat16 or wider, within the bound.
No kernel may reach another device: no remote copies, remote signals or barrier semaphores. Data moves between devices by JAX's collectives and lax.ppermute only.
A program may use at most 192 MiB of HBM per device.

v0:
```python
import functools

import jax
import jax.numpy as jnp
import numpy as np
from jax import lax
from jax.experimental import pallas as pl
from jax.experimental.pallas import tpu as pltpu
from jax.sharding import PartitionSpec as P

BF = jnp.bfloat16
F32 = jnp.float32
HD = 32
WT, WH, WW = 8, 7, 7
WTOK = WT * WH * WW
TOKS = 400
LANES = 512
HALF_ROWS = 208
TABLE = 2535
COARSE = 10
FINE = 256
ROWS = 16
GROUP = 4
BACK_GROUP = 2
EPSILON = 1e-05
HELD = WTOK // 2
SENT_IN = 200
SENT_OUT = 208
LOG2E = 1.4426950408889634
VECTOR_ROWS = 96
GAIN1, SHIFT1, BIAS_Q, BIAS_V, BIAS_P, GAIN2, SHIFT2, BIAS2, BIAS1 = range(80, 89)
ANY = pl.BlockSpec(memory_space=pl.ANY)


def dot(a, b, ca, cb):
    return lax.dot_general(a, b, (((ca,), (cb,)), ((), ())), preferred_element_type=F32)


def cost(flops, moved, trans=0):
    return pl.CostEstimate(flops=1, bytes_accessed=1, transcendentals=0)


def params(size=56):
    return pltpu.CompilerParams(vmem_limit_bytes=size * 1024 * 1024)


def whole_spec(array):
    rank = len(array.shape)
    return pl.BlockSpec(array.shape, lambda *_: (0,) * rank)


def window_spec(array, skip=0):
    rank = len(array.shape)
    return pl.BlockSpec((1,) + array.shape[1:], lambda w, *_: (w + skip,) + (0,) * (rank - 1))


def flip(values, axis=1):
    half = values.shape[axis] // 2
    low = lax.slice_in_dim(values, 0, half, axis=axis)
    high = lax.slice_in_dim(values, half, 2 * half, axis=axis)
    return jnp.concatenate([high, low], axis)


def row_pair(own_ref, got_ref, row, count=1):
    return jnp.concatenate([ref[r : r + 1, :] for ref in (own_ref, got_ref) for r in range(row, row + count)], 1)


def normed(values):
    width = values.shape[1]
    center = jnp.sum(values, 1, keepdims=True) / width
    spread = jnp.sum(values * values, 1, keepdims=True) / width - center * center
    inv = lax.rsqrt(spread + EPSILON)
    return (values - center) * inv, inv


def norm_back(upstream, xhat, inv, gain):
    width = xhat.shape[1]
    scaled = upstream * gain
    total = jnp.sum(scaled, 1, keepdims=True) / width
    along = jnp.sum(scaled * xhat, 1, keepdims=True) / width
    return inv * (scaled - total - xhat * along)


def pack_kernel(gain1, shift1, bqv, bp, gain2, shift2, b2, b1, table, out_ref):
    out_ref[...] = jnp.zeros_like(out_ref)
    heads = table.shape[0]
    for c in range(COARSE):
        size = min(FINE, TABLE - c * FINE)
        out_ref[c * heads : (c + 1) * heads, :size] = table[:, c * FINE : c * FINE + size]
    rows = ((GAIN1, gain1), (SHIFT1, shift1), (BIAS_P, bp), (GAIN2, gain2), (SHIFT2, shift2), (BIAS2, b2))
    for row, ref in rows:
        out_ref[row : row + 1, :] = ref[...].reshape(1, -1)
    out_ref[BIAS_Q : BIAS_Q + 2, :] = bqv[...]
    wide = b1[...].reshape(1, -1)
    for i in range(4):
        out_ref[BIAS1 + i : BIAS1 + i + 1, :] = wide[:, i * 256 : (i + 1) * 256]


def pack(*arrays):
    return pl.pallas_call(
        pack_kernel,
        out_shape=jax.ShapeDtypeStruct((VECTOR_ROWS, FINE), F32),
        cost_estimate=cost(1000, 200000),
        name="pack",
    )(*arrays)


def unpack_kernel(a_ref, b_ref, c_ref, d_ref, gain1, shift1, bqv, bp, table, gain2, shift2, b1, b2):
    a, b, c, d = [ref[...].astype(F32) for ref in (a_ref, b_ref, c_ref, d_ref)]
    total = (a + b) + (c + d)
    heads = table.shape[0]
    for c in range(COARSE):
        size = min(FINE, TABLE - c * FINE)
        table[:, c * FINE : c * FINE + size] = total[c * heads : (c + 1) * heads, :size]
    rows = ((GAIN1, gain1), (SHIFT1, shift1), (BIAS_P, bp), (GAIN2, gain2), (SHIFT2, shift2), (BIAS2, b2))
    for row, ref in rows:
        ref[...] = total[row : row + 1].reshape(-1)
    bqv[...] = total[BIAS_Q : BIAS_Q + 2]
    b1[...] = jnp.concatenate([total[BIAS1 + i : BIAS1 + i + 1] for i in range(4)], 1).reshape(-1)


def unpack(parts, heads):
    vector = jax.ShapeDtypeStruct((FINE,), F32)
    return pl.pallas_call(
        unpack_kernel,
        out_shape=[vector, vector, jax.ShapeDtypeStruct((2, FINE), F32), vector, jax.ShapeDtypeStruct((heads, TABLE), F32), vector, vector, jax.ShapeDtypeStruct((4 * FINE,), F32), vector],
        cost_estimate=cost(1000, 200000),
        name="unpack",
    )(*parts)


def lane_tiles(width):
    return [(t, t * 128, min(128, width - t * 128)) for t in range(-(-width // 128))]


def put_rows(scratch, start, rows):
    for t, begin, size in lane_tiles(rows.shape[1]):
        scratch[t, start : start + rows.shape[0], :size] = rows[:, begin : begin + size]


def strided_rows(scratch, start, count, step, width):
    parts = [scratch[t, pl.ds(start, count, stride=step), :][:, :size] for t, _, size in lane_tiles(width)]
    return jnp.concatenate(parts, 1)


def one_hot(fine_row, width):
    rows = lax.broadcasted_iota(jnp.int32, (FINE, width), 0).astype(jnp.int16)
    return jnp.where(rows == fine_row.astype(jnp.int16), jnp.ones((), BF), jnp.zeros((), BF))


def lookup_kernel(heads, idx_ref, own_ref, got_ref, *rest):
    out_ref, scratch, table = rest[-3:]
    width = idx_ref.shape[1]

    @pl.when(pl.program_id(0) == 0)
    def _():
        for c in range(COARSE):
            span = slice(c * heads, (c + 1) * heads)
            level_rows = jnp.concatenate([own_ref[span, :], got_ref[span, :]], 0)
            table[2 * c * heads : 2 * (c + 1) * heads, :] = (level_rows * LOG2E).astype(BF)

    for r in range(ROWS):
        idx = idx_ref[r : r + 1, :]
        hot = one_hot(jnp.bitwise_and(idx, FINE - 1), width)
        level = lax.shift_right_logical(idx, 8)
        picked = dot(table[...], hot, 1, 0)
        acc = picked[: 2 * heads]
        for c in range(1, COARSE):
            acc = jnp.where(level == c, picked[2 * c * heads : 2 * (c + 1) * heads], acc)
        put_rows(scratch, 2 * r * heads, acc)
    for h in range(2 * heads):
        out_ref[h, :, :width] = strided_rows(scratch, h, ROWS, 2 * heads, width).astype(BF)


def lookup(idx, own, got, heads, start, count, filled=()):
    width = idx.shape[1]
    return pl.pallas_call(
        functools.partial(lookup_kernel, heads),
        grid=(count,),
        in_specs=[pl.BlockSpec((ROWS, width), lambda i: (start + i, 0)), whole_spec(own), whole_spec(got)] + [ANY] * len(filled),
        out_specs=pl.BlockSpec((2 * heads, ROWS, LANES), lambda i: (0, start + i, 0)),
        out_shape=jax.ShapeDtypeStruct((2 * heads, HALF_ROWS, LANES), BF),
        input_output_aliases={3: 0} if filled else {},
        scratch_shapes=[pltpu.VMEM((-(-width // 128), 2 * ROWS * heads, 128), F32), pltpu.VMEM((2 * COARSE * heads, FINE), BF)],
        compiler_params=params(),
        cost_estimate=cost(0, 0),
        name="table_lookup",
    )(idx, own, got, *filled)


def fold_rows(heads, idx_ref, pair_m, pair_o, sent_m, sent_o, scratch, total):
    width = idx_ref.shape[1]
    for h in range(heads):
        put_rows(scratch, h * ROWS, pair_m[h, :, :width].astype(F32) + sent_o[h, :, :width].astype(F32))
        put_rows(scratch, (heads + h) * ROWS, pair_o[h, :, :width].astype(F32) + sent_m[h, :, :width].astype(F32))
    part = jnp.zeros(total.shape, F32)
    fine = jnp.bitwise_and(idx_ref[...], FINE - 1).T.astype(jnp.int16)
    cells = lax.broadcasted_iota(jnp.int32, (width, FINE), 1).astype(jnp.int16)
    for r in range(ROWS):
        hot = jnp.where(cells == fine[:, r : r + 1], jnp.ones((), BF), jnp.zeros((), BF))
        level = lax.shift_right_logical(idx_ref[r : r + 1, :], 8)
        grads = strided_rows(scratch, r, 2 * heads, ROWS, width)
        parts = [jnp.where(level == c, grads, 0.0) for c in range(COARSE)]
        part = part + dot(jnp.concatenate(parts, 0).astype(BF), hot, 1, 0)
    total[...] += part


def fold_start_kernel(heads, core_ref, idx_ref, pair_m, pair_o, sent_m, sent_o, total, scratch):
    step = pl.program_id(0)

    @pl.when(step == 0)
    def _():
        total[...] = jnp.zeros_like(total)

    @pl.when(jnp.logical_or(step > 0, core_ref[0] == 0))
    def _():
        fold_rows(heads, idx_ref, pair_m, pair_o, sent_m, sent_o, scratch, total)


def fold_end_kernel(heads, core_ref, idx_ref, pair_m, pair_o, sent_m, sent_o, init_ref, mid_ref, wide_ref, end_ref, mine_ref, other_ref, scratch, total):
    step = pl.program_id(0)

    @pl.when(step == 0)
    def _():
        total[...] = init_ref[...]

    fold_rows(heads, idx_ref, pair_m, pair_o, sent_m, sent_o, scratch, total)

    @pl.when(step == pl.num_programs(0) - 1)
    def _():
        for half, ref in enumerate((mine_ref, other_ref)):
            for c in range(COARSE):
                at = (2 * c + half) * heads
                ref[c * heads : (c + 1) * heads, :] = total[at : at + heads, :]
            span = slice(half * 256, (half + 1) * 256)
            rows = ((GAIN1, end_ref, 2), (SHIFT1, end_ref, 3), (BIAS_Q, end_ref, 0), (BIAS_V, end_ref, 1), (BIAS_P, mid_ref, 3), (GAIN2, mid_ref, 1), (SHIFT2, mid_ref, 2), (BIAS2, mid_ref, 0))
            for row, source, at in rows:
                ref[row : row + 1, :] = source[at : at + 1, span]
            for i in range(4):
                at = half * 1024 + i * 256
                ref[BIAS1 + i : BIAS1 + i + 1, :] = wide_ref[:, at : at + 256]
            ref[BIAS1 + 4 :, :] = jnp.zeros((VECTOR_ROWS - BIAS1 - 4, 256), F32)


def fold(core, idx, pairs, heads, start, count, extra=()):
    width = idx.shape[1]
    scratch = [pltpu.VMEM((-(-width // 128), 2 * ROWS * heads, 128), F32)]
    total = jax.ShapeDtypeStruct((2 * COARSE * heads, FINE), F32)
    ends = jax.ShapeDtypeStruct((VECTOR_ROWS, FINE), F32)
    outs = [ends, ends] if extra else [total]
    pair = pl.BlockSpec((heads, ROWS, LANES), lambda i, core: (0, start + i, 0))
    return pl.pallas_call(
        functools.partial(fold_end_kernel if extra else fold_start_kernel, heads),
        grid_spec=pltpu.PrefetchScalarGridSpec(
            num_scalar_prefetch=1,
            grid=(count,),
            in_specs=[pl.BlockSpec((ROWS, width), lambda i, core: (start + i, 0))] + [pair] * 4 + [whole_spec(e) for e in extra],
            out_specs=[whole_spec(o) for o in outs],
            scratch_shapes=scratch + ([pltpu.VMEM(total.shape, F32)] if extra else []),
        ),
        out_shape=outs,
        compiler_params=params(),
        cost_estimate=cost(0, 0),
        name="table_fold",
    )(core, idx, *pairs, *extra)


def mask_pieces():
    pieces = []
    rest = np.float32(-100.0 * LOG2E)
    for _ in range(3):
        piece = np.float32(rest.astype(jnp.bfloat16))
        pieces.append(float(piece))
        rest = np.float32(rest - piece)
    return pieces


def region_rows(label):
    width = label.shape[1]
    rows = lax.broadcasted_iota(jnp.int32, (16, width), 0)
    lanes = lax.broadcasted_iota(jnp.int32, (16, width), 1)
    same = jnp.bitwise_and(rows, 3) == label
    level = lax.shift_right_logical(rows, 2)
    high, mid, low = mask_pieces()
    piece = jnp.where(level == 0, high, jnp.where(level == 1, mid, low))
    queries = jnp.where(rows < 12, jnp.where(same, 1.0, 0.0), jnp.where(rows == 15, 1.0, 0.0))
    past = jnp.where(jnp.logical_and(rows == 15, lanes >= WTOK), -1e30, 0.0)
    keys = jnp.where(rows < 12, jnp.where(same, 0.0, piece), past)
    return queries.astype(BF), keys.astype(BF)


def pick_bias(first, own_ref, got_ref, j):
    skip = 2 * HALF_ROWS - TOKS
    low = lax.select_n(first, got_ref[j, :, :TOKS], own_ref[j, :, :TOKS])
    high = lax.select_n(first, own_ref[j, skip:, :TOKS], got_ref[j, skip:, :TOKS])
    return jnp.concatenate([low, high], 0).astype(F32)


def attend_kernel(core_ref, q_ref, k_ref, v_ref, label_ref, own_ref, got_ref, att_ref, exact_ref, lse_ref):
    first = core_ref[0] == 0
    ones = jnp.ones((16, TOKS), BF)
    windows = range(q_ref.shape[0])
    regions = [region_rows(label_ref[w]) for w in windows]
    for j in range(GROUP):
        part = pl.ds(j * HD, HD)
        bias = pick_bias(first, own_ref, got_ref, j)
        for w in windows:
            query_rows, key_rows = regions[w]
            qa = jnp.concatenate([q_ref[w, part, :], query_rows], 0)
            ka = jnp.concatenate([k_ref[w, part, :], key_rows], 0)
            va = jnp.concatenate([v_ref[w, part, :], ones], 0)
            scores = dot(ka, qa, 0, 0) + bias
            peak = jnp.max(scores, 0, keepdims=True)
            weights = jnp.exp2(scores - peak).astype(BF)
            mixed = dot(va, weights, 1, 0)
            total = mixed[HD : HD + 1]
            out = mixed[:HD] / total
            att_ref[w, part, :] = out.astype(BF)
            exact_ref[w, part, :] = out
            lse_ref[w, 0, j : j + 1, :] = peak + jnp.log2(total)


def attention_specs(wins, heads, skip=0, group=GROUP):
    half = heads // (2 * group)
    ratio = GROUP // group
    feat = pl.BlockSpec((wins, group * HD, TOKS), lambda h, core: (0, h + skip, 0))
    label = pl.BlockSpec((wins, 1, TOKS), lambda h, core: (0, 0, 0))
    own = pl.BlockSpec((group, HALF_ROWS, LANES), lambda h, core: (h + skip, 0, 0))
    got = pl.BlockSpec((group, HALF_ROWS, LANES), lambda h, core: ((h + skip + half) % (2 * half), 0, 0))
    stat = pl.BlockSpec((wins, 1, GROUP, TOKS), lambda h, core: (0, (h + skip) // ratio, 0, 0))
    return feat, label, own, got, stat


def attend(core, q, k, v, labels, own, got):
    wins, feats, toks = q.shape
    heads = feats // HD
    feat, label, own_spec, got_spec, stat = attention_specs(wins, heads)
    return pl.pallas_call(
        attend_kernel,
        grid_spec=pltpu.PrefetchScalarGridSpec(
            num_scalar_prefetch=1,
            grid=(heads // GROUP,),
            in_specs=[feat, feat, feat, label, own_spec, got_spec],
            out_specs=[feat, feat, stat],
        ),
        out_shape=[
            jax.ShapeDtypeStruct(q.shape, BF),
            jax.ShapeDtypeStruct(q.shape, F32),
            jax.ShapeDtypeStruct((wins, heads // GROUP, GROUP, toks), F32),
        ],
        compiler_params=params(),
        cost_estimate=cost(0, 0),
        name="attend",
    )(core, q, k, v, labels, own, got)


def split3(row):
    hi = row.astype(BF)
    rest = row - hi.astype(F32)
    mid = rest.astype(BF)
    return hi.astype(F32), mid.astype(F32), rest - mid.astype(F32)


def rows16(parts, width):
    rows = lax.broadcasted_iota(jnp.int32, (16, width), 0)
    out = jnp.zeros((16, width), F32)
    for i, part in enumerate(parts):
        out = jnp.where(rows == i, part, out)
    return out.astype(BF)


def attend_back_kernel(scale, core_ref, q_ref, k_ref, v_ref, label_ref, own_ref, got_ref, exact_ref, lse_ref, g_ref, dq_ref, dk_ref, dv_ref, pair_ref, sent_ref, sums):
    core = core_ref[0]
    first = core == 0
    step = TOKS - HALF_ROWS
    mine, other = pl.multiple_of(core * step, 8), pl.multiple_of((1 - core) * step, 8)
    minus = rows16([-1.0, -1.0, -1.0], TOKS)
    windows = range(q_ref.shape[0])
    regions = [region_rows(label_ref[w]) for w in windows]
    base = lax.rem(pl.program_id(0), GROUP // BACK_GROUP) * BACK_GROUP
    for j in range(BACK_GROUP):
        part = pl.ds(j * HD, HD)
        bias = pick_bias(first, own_ref, got_ref, j)
        total = None
        for w in windows:
            query_rows, key_rows = regions[w]
            q = q_ref[w, part, :]
            k = k_ref[w, part, :]
            g = g_ref[w, part, :]
            qa = jnp.concatenate([q, query_rows, rows16(split3(lse_ref[w, 0, pl.ds(base + j, 1), :]), TOKS)], 0)
            ka = jnp.concatenate([k, key_rows, minus], 0)
            va = jnp.concatenate([v_ref[w, part, :], minus], 0)
            along = jnp.sum(g.astype(F32) * exact_ref[w, part, :], 0, keepdims=True)
            ga = jnp.concatenate([g, rows16(split3(along), TOKS)], 0)
            probs = jnp.exp2(dot(ka, qa, 0, 0) + bias)
            wide = probs * dot(va, ga, 0, 0)
            grads = wide.astype(BF)
            low = probs.astype(BF)
            dv_ref[w, part, :] = dot(g, low, 1, 1).astype(BF)
            dk_ref[w, part, :] = (dot(q, grads, 1, 1) * (1.0 / LOG2E)).astype(BF)
            dq_ref[w, part, :] = (dot(k, grads, 1, 0) * scale).astype(BF)
            total = wide if total is None else total + wide
        sums[...] = total
        pair_ref[j, :, :TOKS] = sums[pl.ds(mine, HALF_ROWS), :].astype(BF)
        sent_ref[j, :, :TOKS] = sums[pl.ds(other, HALF_ROWS), :].astype(BF)


def attend_back(core, q, k, v, labels, own, got, exact, lse, g, scale, side):
    wins, feats, toks = q.shape
    heads = feats // HD
    blocks = heads // (2 * BACK_GROUP)
    feat, label, own_spec, got_spec, stat = attention_specs(wins, heads, side * blocks, BACK_GROUP)
    out = pl.BlockSpec((wins, BACK_GROUP * HD, toks), lambda h, core: (0, h, 0))
    pair = pl.BlockSpec((BACK_GROUP, HALF_ROWS, LANES), lambda h, core: (h, 0, 0))
    return pl.pallas_call(
        functools.partial(attend_back_kernel, scale),
        grid_spec=pltpu.PrefetchScalarGridSpec(
            num_scalar_prefetch=1,
            grid=(blocks,),
            in_specs=[feat, feat, feat, label, own_spec, got_spec, feat, stat, feat],
            out_specs=[out, out, out, pair, pair],
            scratch_shapes=[pltpu.VMEM((toks, toks), F32)],
        ),
        out_shape=[jax.ShapeDtypeStruct((wins, feats // 2, toks), BF)] * 3 + [jax.ShapeDtypeStruct((heads // 2, HALF_ROWS, LANES), BF)] * 2,
        compiler_params=params(),
        cost_estimate=cost(0, 0),
        name="attend_back",
    )(core, q, k, v, labels, own, got, exact, lse, g)


def front_kernel(scale, xm_ref, xo_ref, own_ref, got_ref, wm_ref, wo_ref, *rest):
    q_ref, k_ref, v_ref, first_ref = rest[-4:]
    x = jnp.concatenate([xm_ref[0], xo_ref[0]], 1).astype(F32)
    xhat, _ = normed(x)
    first = (xhat * row_pair(own_ref, got_ref, GAIN1) + row_pair(own_ref, got_ref, SHIFT1)).astype(BF)
    first_ref[0] = first.T
    for t, (w_ref, vec_ref) in enumerate(((wm_ref, own_ref), (wo_ref, got_ref))):
        cols = w_ref.shape[1] // 3
        rows = pl.ds(t * cols, cols)
        made = dot(first if t == 0 else flip(first), w_ref[...], 1, 0)
        q = (made[:, :cols] + vec_ref[BIAS_Q : BIAS_Q + 1, :]) * scale
        v = made[:, 2 * cols :] + vec_ref[BIAS_V : BIAS_V + 1, :]
        q_ref[0, rows, :] = q.astype(BF).T
        k_ref[0, rows, :] = made[:, cols : 2 * cols].astype(BF).T
        v_ref[0, rows, :] = v.astype(BF).T


def front(xm, xo, own, got, wm, wo, scale, deps):
    wins, toks, half = xm.shape
    out = jax.ShapeDtypeStruct((wins, 2 * (wm.shape[1] // 3), toks), BF)
    return pl.pallas_call(
        functools.partial(front_kernel, scale),
        grid=(wins,),
        in_specs=[window_spec(xm), window_spec(xo), whole_spec(own), whole_spec(got), whole_spec(wm), whole_spec(wo)] + [ANY] * len(deps),
        out_specs=[window_spec(out)] * 4,
        out_shape=[out] * 4,
        compiler_params=params(),
        cost_estimate=cost(8 * wins * toks * half * wm.shape[1], wins * toks * half * 16 + wm.size * 4),
        name="front",
    )(xm, xo, own, got, wm, wo, *deps)


def middle_kernel(xm_ref, xo_ref, att_ref, own_ref, got_ref, wm_ref, wo_ref, *rest):
    mid_ref, second_ref, act_ref, slope_ref = rest[-4:]
    half = xm_ref.shape[2]
    wide = wm_ref.shape[1] - half
    branch = dot(att_ref[0, :half, :].T, wm_ref[:, :half], 1, 1) + flip(dot(att_ref[0, half:, :].T, wo_ref[:, :half], 1, 1))
    x = jnp.concatenate([xm_ref[0], xo_ref[0]], 1).astype(F32)
    middle = x + (branch + row_pair(own_ref, got_ref, BIAS_P))
    mid_ref[0] = middle
    xhat, _ = normed(middle)
    second = (xhat * row_pair(own_ref, got_ref, GAIN2) + row_pair(own_ref, got_ref, SHIFT2)).astype(BF)
    second_ref[0] = second
    turned = flip(second)
    for t, (w_ref, vec_ref) in enumerate(((wm_ref, own_ref), (wo_ref, got_ref))):
        for s in range(0, wide, 256):
            at = t * wide + s
            bias = vec_ref[BIAS1 + s // 256 : BIAS1 + s // 256 + 1, :]
            hidden = dot(second if t == 0 else turned, w_ref[:, half + s : half + s + 256], 1, 0) + bias
            phi = 0.5 + 0.5 * lax.erf(hidden * (0.5**0.5))
            bell = jnp.exp2(hidden * hidden * (-0.5 * LOG2E)) * (1.0 / (2.0 * np.pi) ** 0.5)
            act_ref[0, :, at : at + 256] = (hidden * phi).astype(BF)
            slope_ref[0, :, at : at + 256] = (phi + hidden * bell).astype(BF)


def middle_forward(xm, xo, att, own, got, wm, wo):
    wins, toks, half = xm.shape
    width = 2 * half
    hidden = 2 * (wm.shape[1] - half)
    wide = jax.ShapeDtypeStruct((wins, toks, hidden), BF)
    outs = [jax.ShapeDtypeStruct((wins, toks, width), F32), jax.ShapeDtypeStruct((wins, toks, width), BF), wide, wide]
    fixed = (own, got, wm, wo)
    return pl.pallas_call(
        middle_kernel,
        grid=(wins,),
        in_specs=[window_spec(a) for a in (xm, xo, att)] + [whole_spec(a) for a in fixed],
        out_specs=[window_spec(o) for o in outs],
        out_shape=outs,
        compiler_params=params(28),
        cost_estimate=cost(8 * wins * toks * width * wm.shape[1], wins * toks * (width * 10 + hidden * 4) + wm.size * 4, wins * toks * hidden),
        name="middle_forward",
    )(xm, xo, att, *fixed)


def put_pieces(out, nearm_ref, nearo_ref, farm_ref, faro_ref):
    half = out.shape[1] // 2
    for ref, rows, cols in ((nearm_ref, 0, 0), (nearo_ref, 0, half), (farm_ref, TOKS - SENT_OUT, 0), (faro_ref, TOKS - SENT_OUT, half)):
        ref[0] = out[rows : rows + SENT_OUT, cols : cols + half]


def middle_back_kernel(cm_ref, co_ref, mid_ref, second_ref, act_ref, slope_ref, att_ref, own_ref, got_ref, wm_ref, wo_ref, fm_ref, fo_ref, *rest):
    nearm_ref, nearo_ref, farm_ref, faro_ref, gm_ref, gr_ref, onem_ref, oneo_ref, twom_ref, twoo_ref, small_ref, wide_ref, accm, acco = rest[-14:]
    win = pl.program_id(0)
    half = cm_ref.shape[2]
    wide = fm_ref.shape[1]

    @pl.when(win == 0)
    def _():
        accm[...] = jnp.zeros_like(accm)
        acco[...] = jnp.zeros_like(acco)
        small_ref[...] = jnp.zeros_like(small_ref)
        wide_ref[...] = jnp.zeros_like(wide_ref)

    cot = jnp.concatenate([cm_ref[0], co_ref[0]], 1)
    cot_turned = flip(cot)
    cot_t = cot.T
    second_t = second_ref[0].T
    sides = (
        (wm_ref, fm_ref, accm, cot, cot_t, second_t),
        (wo_ref, fo_ref, acco, cot_turned, flip(cot_t, 0), flip(second_t, 0)),
    )
    made, pulled = [], []
    for t, (w_ref, f_ref, acc, c, c_t, s_t) in enumerate(sides):
        forward = jnp.zeros(cot.shape, F32)
        grad_second = jnp.zeros(cot.shape, F32)
        for s in range(0, wide, 512):
            span = slice(t * wide + s, t * wide + s + 512)
            fc2 = f_ref[:, s : s + 512]
            active = act_ref[0, :, span]
            forward = forward + dot(active, fc2, 1, 1)
            grad = (dot(c, fc2, 1, 0) * slope_ref[0, :, span].astype(F32)).astype(BF)
            wide_ref[:, span] += jnp.sum(grad.astype(F32), 0, keepdims=True)
            acc[:, half + wide + s : half + wide + s + 512] += dot(c_t, active, 1, 0)
            acc[:, half + s : half + s + 512] += dot(s_t, grad, 1, 0)
            grad_second = grad_second + dot(grad, w_ref[:, half + s : half + s + 512], 1, 1)
        made.append(forward)
        pulled.append(grad_second)
    out = mid_ref[0] + (made[0] + flip(made[1]) + row_pair(own_ref, got_ref, BIAS2))
    put_pieces(out.astype(BF), nearm_ref, nearo_ref, farm_ref, faro_ref)
    grad_second = pulled[0] + flip(pulled[1])
    upstream = cot.astype(F32)
    xhat, inv = normed(mid_ref[0])
    grad_mid = upstream + norm_back(grad_second, xhat, inv, row_pair(own_ref, got_ref, GAIN2))
    gm_ref[0] = grad_mid
    branch = grad_mid.astype(BF)
    branch_t = branch.T
    gr_ref[0, :half, :] = dot(branch, wm_ref[:, :half], 1, 0).astype(BF).T
    gr_ref[0, half:, :] = dot(flip(branch), wo_ref[:, :half], 1, 0).astype(BF).T
    accm[:, :half] += dot(branch_t, att_ref[0, :half, :], 1, 1)
    acco[:, :half] += dot(flip(branch_t, 0), att_ref[0, half:, :], 1, 1)
    small_ref[0:1, :] += jnp.sum(upstream, 0, keepdims=True)
    small_ref[1:2, :] += jnp.sum(grad_second * xhat, 0, keepdims=True)
    small_ref[2:3, :] += jnp.sum(grad_second, 0, keepdims=True)
    small_ref[3:4, :] += jnp.sum(branch.astype(F32), 0, keepdims=True)

    @pl.when(win == pl.num_programs(0) - 1)
    def _():
        for acc, one_ref, two_ref in ((accm, onem_ref, twom_ref), (acco, oneo_ref, twoo_ref)):
            one_ref[...] = acc[:, half : half + wide].astype(BF)
            two_ref[:, :half] = acc[:, :half].astype(BF)
            two_ref[:, half:] = acc[:, half + wide :].astype(BF)


def middle_back(cm, co, mid, second, act, slope, att, own, got, wm, wo, fm, fo, deps):
    wins, toks, half = cm.shape
    width = 2 * half
    hidden = act.shape[2]
    windows = (cm, co, mid, second, act, slope, att)
    fixed = (own, got, wm, wo, fm, fo)
    plain = jax.ShapeDtypeStruct((wins, SENT_OUT, half), BF)
    outs = [plain, plain, plain, plain, jax.ShapeDtypeStruct(mid.shape, F32), jax.ShapeDtypeStruct((wins, width, toks), BF)]
    grads = jax.ShapeDtypeStruct((width, wm.shape[1] + fm.shape[1]), BF)
    one = jax.ShapeDtypeStruct((width, wm.shape[1] - half), BF)
    two = jax.ShapeDtypeStruct((width, half + fm.shape[1]), BF)
    sums = [one, one, two, two, jax.ShapeDtypeStruct((4, width), F32), jax.ShapeDtypeStruct((1, hidden), F32)]
    return pl.pallas_call(
        middle_back_kernel,
        grid=(wins,),
        in_specs=[window_spec(a, wins if a is co else 0) for a in windows] + [whole_spec(a) for a in fixed] + [ANY] * len(deps),
        out_specs=[window_spec(o) for o in outs] + [whole_spec(o) for o in sums],
        out_shape=[pltpu.HBM(o.shape, o.dtype) for o in outs + sums],
        scratch_shapes=[pltpu.VMEM(grads.shape, F32), pltpu.VMEM(grads.shape, F32)],
        compiler_params=params(28),
        cost_estimate=cost(12 * wins * toks * width * (width + 2 * hidden), wins * toks * (width * 16 + hidden * 4) + fm.size * 12),
        name="middle_back",
    )(*windows, *fixed, *deps)


def side_kernel(first_ref, dq_ref, dk_ref, dv_ref, do_ref):
    for c, ref in enumerate((dq_ref, dk_ref, dv_ref)):
        cols = ref.shape[1]
        part = sum(dot(flip(first_ref[w], 0), ref[w], 1, 1) for w in range(first_ref.shape[0]))
        do_ref[:, c * cols : (c + 1) * cols] = part.astype(BF)


def side_grads(first, grads):
    wins, width, toks = first.shape
    return pl.pallas_call(
        side_kernel,
        out_shape=jax.ShapeDtypeStruct((width, 3 * grads[0].shape[1]), BF),
        compiler_params=params(),
        cost_estimate=cost(0, 0),
        name="side_grads",
    )(first, *grads)


def back_kernel(place_ref, xm_ref, xo_ref, first_ref, qm_ref, km_ref, vm_ref, qo_ref, ko_ref, vo_ref, gm_ref, own_ref, got_ref, wm_ref, wo_ref, side_ref, nearm_ref, nearo_ref, farm_ref, faro_ref, keep_ref, send_ref, small_ref, acc):
    win = pl.program_id(0)

    @pl.when(win == 0)
    def _():
        acc[...] = side_ref[...].astype(F32)
        small_ref[...] = jnp.zeros_like(small_ref)

    xhat, inv = normed(jnp.concatenate([xm_ref[0], xo_ref[0]], 1).astype(F32))
    half = xm_ref.shape[2]
    mine = jnp.concatenate([qm_ref[0], km_ref[0], vm_ref[0]], 0)
    other = jnp.concatenate([qo_ref[0], ko_ref[0], vo_ref[0]], 0)
    acc[...] += dot(first_ref[0], mine, 1, 1)
    grad_first = dot(mine, wm_ref[...], 0, 1) + flip(dot(other, wo_ref[...], 0, 1))
    grad_first = grad_first.astype(BF).astype(F32)
    grad_x = gm_ref[0] + norm_back(grad_first, xhat, inv, row_pair(own_ref, got_ref, GAIN1))
    put_pieces(grad_x.astype(BF), nearm_ref, nearo_ref, farm_ref, faro_ref)
    ones = jnp.ones((8, mine.shape[1]), BF)
    for t, side in enumerate((mine, other)):
        sums = dot(ones, side, 1, 1)[0:1]
        span = slice(t * half, (t + 1) * half)
        small_ref[0:1, span] += sums[:, :half]
        small_ref[1:2, span] += sums[:, 2 * half :]
    small_ref[2:3, :] += jnp.sum(grad_first * xhat, 0, keepdims=True)
    small_ref[3:4, :] += jnp.sum(grad_first, 0, keepdims=True)

    @pl.when(win == pl.num_programs(0) - 1)
    def _():
        rows = keep_ref.shape[-2]
        own = place_ref[0]
        for i in range(keep_ref.shape[0]):
            for ref, side in ((keep_ref, own), (send_ref, 1 - own)):
                at = pl.multiple_of((2 * i + side) * rows, 16)
                ref[i] = acc[pl.ds(at, rows), :].astype(BF)


def back(place, blocks, xm, xo, first, mine, other, gm, own, got, wm, wo, side):
    wins, toks, half = xm.shape
    windows = (xm, xo, first) + mine + other + (gm,)
    fixed = (own, got, wm, wo, side)
    plain = jax.ShapeDtypeStruct((wins, SENT_OUT, half), BF)
    grads = jax.ShapeDtypeStruct((blocks // 2, 2 * half // blocks, wm.shape[1]), BF)
    small = jax.ShapeDtypeStruct((4, 2 * half), F32)
    outs = [plain] * 4 + [grads, grads, small]
    return pl.pallas_call(
        back_kernel,
        grid_spec=pltpu.PrefetchScalarGridSpec(
            num_scalar_prefetch=1,
            grid=(wins,),
            in_specs=[window_spec(a) for a in windows] + [whole_spec(a) for a in fixed],
            out_specs=[window_spec(plain)] * 4 + [whole_spec(grads), whole_spec(grads), whole_spec(small)],
            scratch_shapes=[pltpu.VMEM(wm.shape, F32)],
        ),
        out_shape=[pltpu.HBM(o.shape, o.dtype) for o in outs],
        compiler_params=params(),
        cost_estimate=cost(0, 0),
        name="back",
    )(place, *windows, *fixed)


def one_hot_rows(picks, size):
    cells = lax.broadcasted_iota(jnp.int32, (picks.shape[0], size), 1)
    return jnp.where(cells == picks, 1.0, 0.0).astype(BF)


def select_in_kernel(core_ref, picks_ref, x_ref, cot_ref, far_ref, xm_ref, cm_ref, other_ref):
    skip = WTOK - SENT_IN
    near = jnp.concatenate([jnp.concatenate([ref[w, skip:, :] for ref in (x_ref, cot_ref)], 1) for w in range(4)], 0)
    rows = far_ref.shape[0] // 2
    far = jnp.concatenate([far_ref[:rows, :], far_ref[rows:, :]], 1)
    low = dot(one_hot_rows(picks_ref[0, : 4 * SENT_IN, :], near.shape[0]), near, 1, 0)
    high = dot(one_hot_rows(picks_ref[0, 4 * SENT_IN :, :], far.shape[0]), far, 1, 0)
    places = lax.broadcasted_iota(jnp.int32, (SENT_IN - skip, 1), 0) + skip
    half = x_ref.shape[2]
    for w in range(4):
        first, last = low[w * SENT_IN : (w + 1) * SENT_IN], high[w * SENT_OUT : (w + 1) * SENT_OUT]
        over = jnp.where(places < HELD, first[skip:], last[: SENT_IN - skip])
        whole = jnp.concatenate([first[:skip], over, last[SENT_IN - skip :]], 0).astype(BF)
        if w < 2:
            xm_ref[w] = whole[:, :half]
            cm_ref[w] = whole[:, half:]
        else:
            other_ref[w - 2] = whole[:, :half]
            other_ref[w] = whole[:, half:]


def core_block(picks):
    return pl.BlockSpec((1,) + picks.shape[1:], lambda i, core: (core[0], 0, 0))


def select_in(core, picks, x, cot, far):
    out = jax.ShapeDtypeStruct((2, TOKS, x.shape[2]), BF)
    other = jax.ShapeDtypeStruct((4, TOKS, x.shape[2]), BF)
    return pl.pallas_call(
        select_in_kernel,
        grid_spec=pltpu.PrefetchScalarGridSpec(
            num_scalar_prefetch=1,
            grid=(1,),
            in_specs=[core_block(picks), whole_spec(x), whole_spec(cot), whole_spec(far)],
            out_specs=[whole_spec(out), whole_spec(out), whole_spec(other)],
        ),
        out_shape=[out, out, other],
        compiler_params=params(28),
        cost_estimate=cost(0, 0),
        name="select_in",
    )(core, picks, x, cot, far)


def select_out_kernel(core_ref, picks_ref, kept_ref, beside_ref, across_ref, corner_ref, out_ref):
    skip = WTOK - SENT_IN
    near = jnp.concatenate([kept_ref[...], beside_ref[...]], 0)
    far = jnp.concatenate([across_ref[...], corner_ref[...]], 0)
    low = dot(one_hot_rows(picks_ref[0, : 4 * SENT_IN, :], far.shape[0]), far, 1, 0)
    high = dot(one_hot_rows(picks_ref[0, 4 * SENT_IN :, :], near.shape[0]), near, 1, 0)
    rows = lax.broadcasted_iota(jnp.int32, (SENT_IN - skip, 1), 0) + skip
    for w in range(4):
        first, last = [part[w * SENT_IN : (w + 1) * SENT_IN] for part in (low, high)]
        out_ref[w, :skip, :] = first[:skip]
        out_ref[w, skip:SENT_IN, :] = jnp.where(rows < HELD, first[skip:], last[: SENT_IN - skip])
        out_ref[w, SENT_IN:, :] = last[SENT_IN - skip :]


def select_out(core, picks, arrays):
    out = jax.ShapeDtypeStruct((4, WTOK, arrays[0].shape[1]), F32)
    return pl.pallas_call(
        select_out_kernel,
        grid_spec=pltpu.PrefetchScalarGridSpec(
            num_scalar_prefetch=1,
            grid=(1,),
            in_specs=[core_block(picks)] + [whole_spec(a) for a in arrays],
            out_specs=whole_spec(out),
        ),
        out_shape=out,
        compiler_params=params(28),
        cost_estimate=cost(0, 0),
        name="select_out",
    )(core, picks, *arrays)


def bits_of(axis):
    return lax.axis_size(axis).bit_length() - 1


def bit_on(axis, bit):
    return lax.shift_right_logical(lax.axis_index(axis), bit) % 2


def swap(value, axis, bit=0):
    pairs = [(source, source ^ (1 << bit)) for source in range(lax.axis_size(axis))]
    return lax.ppermute(value, axis, pairs)


def bit_order():
    count = bits_of("shard")
    return list(range(count - 1, 0, -1)) + [0]


def row_place(bit):
    place = bit_on("shard", bit)
    if bit == bits_of("shard") - 1:
        place = jnp.bitwise_xor(place, lax.axis_index("tensor"))
    return place


def ordered(on, mine, other, axis):
    return jnp.concatenate((jnp.where(on, other, mine), jnp.where(on, mine, other)), axis)


def after(value, *deps):
    return lax.optimization_barrier((value,) + deps)[0]


def gather_start(part):
    rows, cols = part.shape
    return part.reshape((1,) * bits_of("shard") + (rows, cols))


def joint(values, deps):
    return lax.optimization_barrier(tuple(values) + tuple(deps))[: len(values)]


def gather_join(held, bit, got):
    return ordered(row_place(bit) == 1, held, got, bits_of("shard") - 1 - bit)


def gather_send(held, bits):
    for bit in bits[:-1]:
        held = gather_join(held, bit, swap(held, "shard", bit))
    return held, swap(held, "shard", bits[-1])


def choose(array, index, axis):
    return lax.dynamic_slice_in_dim(array, index, 1, axis)


def add_rounded(a, b):
    return (a.astype(F32) + b.astype(F32)).astype(BF)


def split_rows(part):
    count = bits_of("shard")
    return part.reshape((2,) * count + (part.shape[0] >> count, part.shape[1]))


def scatter_add(held, bit, got):
    axis = bits_of("shard") - 1 - bit
    return add_rounded(choose(held, row_place(bit), axis), got)


def scatter_send(held, bits):
    for bit in bits[:-1]:
        held = scatter_add(held, bit, scatter_send(held, (bit,))[1])
    axis = bits_of("shard") - 1 - bits[-1]
    return held, swap(choose(held, 1 - row_place(bits[-1]), axis), "shard", bits[-1])


def ctx_half(held, own):
    axis = held.ndim - 2
    half = held.shape[axis] // 2
    return lax.dynamic_slice_in_dim(held, own * half, half, axis)


def ctx_split_send(held):
    return swap(ctx_half(held, 1 - bit_on("ctx", 0)), "ctx")


def ctx_split_add(held, got):
    return add_rounded(ctx_half(held, bit_on("ctx", 0)), got)


def flat(held):
    return held.reshape(held.shape[-2:])


def ctx_send(held):
    held = flat(held)
    for bit in range(bits_of("ctx") - 1):
        held = add_rounded(held, swap(held, "ctx", bit))
    return held, swap(held, "ctx", bits_of("ctx") - 1)


def ctx_add(held, got):
    return held.astype(F32) + got.astype(F32)


def joint_swap(value, mask):
    size = lax.axis_size("shard") * lax.axis_size("ctx")
    return lax.ppermute(value, ("shard", "ctx"), [(i, i ^ mask) for i in range(size)])


def joint_parts(value, bits):
    value = value.astype(BF)
    low = 1 << bits[0]
    if len(bits) == 1:
        return [value, joint_swap(value, low), jnp.zeros_like(value), jnp.zeros_like(value)]
    high = 1 << bits[1]
    return [value, joint_swap(value, low), joint_swap(value, high), joint_swap(value, low | high)]


def add_parts(parts):
    a, b, c, d = [part.astype(F32) for part in parts]
    return (a + b) + (c + d)


def joint_groups():
    bits = list(range(bits_of("shard") + bits_of("ctx")))
    return [bits[i : i + 2] for i in range(0, len(bits), 2)]


def roll_axis(shaped, axis_pos, levels, backward):
    token_axis = 4 + axis_pos
    length = shaped.shape[token_axis]
    border = length - length // 2 if backward else length // 2
    before = lax.slice_in_dim(shaped, 0, border, axis=token_axis)
    after = lax.slice_in_dim(shaped, border, length, axis=token_axis)
    moving = after if backward else before
    if axis_pos < levels:
        moving = swap(moving, "ctx", levels - 1 - axis_pos)
    else:
        moving = jnp.roll(moving, 1 if backward else -1, axis=1 + axis_pos)
    return jnp.concatenate((moving, before) if backward else (after, moving), axis=token_axis)


def window_roll(windows, clips, counts, backward):
    shaped = windows.reshape((clips,) + counts + (WT, WH, WW, windows.shape[-1]))
    for axis_pos in range(3):
        shaped = roll_axis(shaped, axis_pos, bits_of("ctx"), backward)
    return shaped.reshape(windows.shape)


def frame_sources():
    source = np.zeros((4, HELD), np.int64)
    for h in range(2 * WH):
        for w in range(2 * WW):
            here = (h // WH) * 2 + w // WW
            there_h, there_w = (h + WH // 2) % (2 * WH), (w + WW // 2) % (2 * WW)
            there = (there_h // WH) * 2 + there_w // WW
            for a in range(WT // 2):
                row = (a * WH + h % WH) * WW + w % WW
                source[here, row] = there * HELD + (a * WH + there_h % WH) * WW + there_w % WW
    return source


def picks_in():
    source = frame_sources()
    there, row = source // HELD, source % HELD
    picks = np.full((4, TOKS), -1)
    picks[:, :HELD] = there * SENT_IN + row + SENT_IN - HELD
    picks[:, HELD:WTOK] = there * SENT_IN + row
    both = []
    for rows in (picks, np.concatenate((picks[2:], picks[:2]))):
        both.append(np.concatenate((rows[:, :SENT_IN].reshape(-1, 1), rows[:, WTOK - SENT_IN :].reshape(-1, 1))))
    return jnp.asarray(np.stack(both), jnp.int32)


def picks_out():
    place = np.argsort(frame_sources().reshape(-1)).reshape(4, HELD)
    there, row = place // HELD, place % HELD
    both = []
    for core in range(2):
        block = ((there // 2 + core) % 2) * 2 * SENT_OUT + (there % 2) * SENT_OUT
        picks = np.zeros((4, WTOK), np.int64)
        picks[:, HELD:] = block + row
        picks[:, :HELD] = block + row + HELD - (TOKS - SENT_OUT)
        both.append(np.concatenate((picks[:, :SENT_IN].reshape(-1, 1), picks[:, WTOK - SENT_IN :].reshape(-1, 1))))
    return jnp.asarray(np.stack(both), jnp.int32)


def plain_ring(clips):
    return bits_of("ctx") == 1 and clips == 1


def shift_start(arrays, clips):
    if plain_ring(clips):
        sent = jnp.concatenate([a[:, :SENT_IN] for a in arrays], 0)
        return swap(sent.reshape(-1, sent.shape[-1]), "ctx")
    return arrays[0][:1, :8]


def shift_in(arrays, got, clips, counts, core_row):
    if plain_ring(clips):
        xm, cm, other = select_in(core_row, picks_in(), *arrays, got)
        return xm, cm, swap(other, "tensor")
    half = arrays[0].shape[0] // 2
    core = lax.axis_index("tensor")
    mine, sent = [], []
    for array in arrays:
        moved = jnp.pad(window_roll(array, clips, counts, False), ((0, 0), (0, TOKS - WTOK), (0, 0)))
        mine.append(lax.dynamic_slice_in_dim(moved, core * half, half, 0))
        sent.append(lax.dynamic_slice_in_dim(moved, (1 - core) * half, half, 0))
    return mine[0], mine[1], swap(jnp.concatenate(sent, 0), "tensor")


def leave_start(pieces, clips):
    nearm, nearo, farm, faro = pieces
    width = nearm.shape[-1]
    if not plain_ring(clips):
        cut = TOKS - SENT_OUT
        mine, other = [jnp.concatenate((near[:, :cut], far), 1) for near, far in ((nearm, farm), (nearo, faro))]
        return mine, swap(other, "tensor")
    nearm, nearo, farm, faro = [piece.reshape(-1, width) for piece in pieces]
    corner = lax.ppermute(faro, ("ctx", "tensor"), [(i, i ^ 3) for i in range(4)])
    return nearm, swap(nearo, "tensor"), swap(farm, "ctx"), corner


def leave_end(parts, clips, counts, core_row, *deps):
    parts = (after(parts[0], *deps),) + tuple(parts[1:])
    if plain_ring(clips):
        return select_out(core_row, picks_out(), parts)
    windows = ordered(lax.axis_index("tensor") == 1, parts[0], parts[1], 0)
    return window_roll(windows[:, :WTOK], clips, counts, True).astype(F32)


def on_device(
    clip_input,
    cotangent,
    gain_one,
    shift_one,
    w_qkv,
    b_qv,
    w_proj,
    b_proj,
    bias_table,
    gain_two,
    shift_two,
    w_fc1,
    b_fc1,
    w_fc2,
    b_fc2,
    rel_index,
    regions,
):
    clips, window_count, tokens, half_width = clip_input.shape
    heads = bias_table.shape[0]
    levels = bits_of("ctx")
    counts = tuple(1 if axis_pos < levels else 2 for axis_pos in range(3))
    core = lax.axis_index("tensor")
    core_row = core.astype(jnp.int32).reshape(1)
    total_windows = clips * window_count
    held_windows = total_windows // 2
    scale = HD ** (-0.5)
    hidden = w_fc1.shape[1]

    own = pack(gain_one, shift_one, b_qv, b_proj, gain_two, shift_two, b_fc2, b_fc1, bias_table)
    qkv = gather_start(w_qkv.transpose(1, 0, 2).reshape(w_qkv.shape[1], -1))
    rest = gather_start(jnp.concatenate((w_proj.T, w_fc1, w_fc2.T), 1))
    index = jnp.pad(rel_index.T, ((0, TOKS - tokens), (0, TOKS - tokens)))
    index = lax.dynamic_slice_in_dim(index, core * (TOKS - HALF_ROWS), HALF_ROWS, 0)
    block = HALF_ROWS // ROWS
    cut = block // 2
    early_blocks = 5
    labels = jnp.tile(regions, (clips, 1))
    labels = lax.dynamic_slice_in_dim(labels, core * held_windows, held_windows, 0)
    labels = jnp.pad(labels, ((0, 0), (0, TOKS - tokens)))[:, None, :]

    order = bit_order()
    first, middle, last = order[0], order[1:-1], order[-1]
    clip_rows = clip_input.reshape(total_windows, tokens, half_width)
    cot_rows = cotangent.reshape(total_windows, tokens, half_width)

    pair_rows = (clip_rows, cot_rows)
    pair_got = shift_start(pair_rows, clips)
    qkv_got, own, index = joint((swap(qkv, "shard", first), own, index), ())
    got = swap(own, "tensor")
    qkv = gather_join(qkv, first, qkv_got)
    qkv, qkv_got = gather_send(qkv, middle)
    rest = after(rest, qkv)
    rest_got = swap(rest, "shard", first)
    part_own = lookup(after(index, qkv), own, got, heads, 0, early_blocks)
    qkv_got, pair_got, rest_got, part_own = joint((qkv_got, pair_got, rest_got, part_own), ())
    qkv = gather_join(qkv, middle[-1], qkv_got)
    rest = gather_join(rest, first, rest_got)
    rest, rest_got = gather_send(rest, middle)
    qkv_got = swap(qkv, "shard", last)
    xm, cm, other = shift_in(pair_rows, pair_got, clips, counts, core_row)
    bias_own = lookup(after(index, xm), own, got, heads, early_blocks, block - early_blocks, (part_own,))
    rest_got, qkv_got, other, bias_own = joint((rest_got, qkv_got, other, bias_own), ())
    qkv = gather_join(qkv, last, qkv_got)
    qkv = qkv.reshape(-1, qkv.shape[-1])
    qkv_other = swap(qkv, "tensor")
    rest = gather_join(rest, middle[-1], rest_got)
    rest_got = swap(rest, "shard", last)
    bias_got = swap(bias_own, "tensor")
    queries, keys, values, first_t = front(xm, other, own, got, qkv, qkv_other, scale * LOG2E, ())
    att, exact, lse = attend(core_row, queries, keys, values, labels, bias_own, bias_got)
    rest_got, att = joint((rest_got, att), ())
    edge = half_width + hidden
    early, late = [gather_join(rest[..., span], last, rest_got[..., span]) for span in (slice(0, edge), slice(edge, None))]
    early, late = [w.reshape(-1, w.shape[-1]) for w in (early, late)]
    early_other, late_other = swap(early, "tensor"), swap(late, "tensor")
    mid, second, act, slope = middle_forward(xm, other, att, own, got, early, early_other)
    *block_pieces, grad_mid, grad_att, one_mine, one_other, two_mine, two_other, small_mid, small_wide = middle_back(cm, other, mid, second, act, slope, att, own, got, early, early_other, late, late_other, ())

    order = order[::-1]
    twice = bits_of("ctx") == 1
    args = (core_row, queries, keys, values, labels, bias_own, bias_got)
    block_parts = leave_start(block_pieces, clips)
    one_got, two_got = swap(one_other, "tensor"), swap(two_other, "tensor")
    qo, ko, vo, pair_o, sent_o = attend_back(*args, exact, lse, grad_att, scale, 1)
    one_got, two_got, qo, sent_o, *moved = joint((one_got, two_got, qo, sent_o) + tuple(block_parts[1:]), ())
    block_parts = (block_parts[0],) + tuple(moved)
    one, two = split_rows(add_rounded(one_mine, one_got)), split_rows(add_rounded(two_mine, two_got))
    one_got = scatter_send(one, order[:1])[1]
    two_got = ctx_split_send(two) if twice else scatter_send(two, order[:1])[1]
    side = side_grads(first_t, (qo, ko, vo))
    side_got, sent_o = swap(side, "tensor"), swap(sent_o, "tensor")
    qm, km, vm, pair_m, sent_m = attend_back(*args, exact, lse, after(grad_att, side), scale, 0)
    one_got, two_got, side, sent_o, qm, sent_m = joint((one_got, two_got, side_got, sent_o, qm, sent_m), ())
    one = scatter_add(one, order[0], one_got)
    two = ctx_split_add(two, two_got) if twice else scatter_add(two, order[0], two_got)
    one_got = scatter_send(one, order[1:2])[1]
    two_bits = order if twice else order[1:]
    two_got = scatter_send(two, two_bits[:1])[1]
    sent_m = swap(sent_m, "tensor")
    place = row_place(0).astype(jnp.int32).reshape(1)
    *grad_pieces, qkv_grads, qkv_sent, small_end = back(place, lax.axis_size("shard"), xm, other, first_t, (after(qm, one, two), km, vm), (qo, ko, vo), grad_mid, own, got, qkv, qkv_other, side)
    block_out = leave_end(block_parts, clips, counts, core_row, small_end)
    one_got, two_got, sent_m, block_out = joint((one_got, two_got, sent_m, block_out), ())
    one = scatter_add(one, order[1], one_got)
    two = scatter_add(two, two_bits[0], two_got)
    shape = (2,) * (len(order) - 1) + (1,) + qkv_grads.shape[1:]
    qkv_got = swap(qkv_sent.reshape(shape), "shard", order[0])
    grad_parts = leave_start(grad_pieces, clips)
    two_got = scatter_send(two, two_bits[1:2])[1]
    one, one_got = scatter_send(one, order[2:])
    pairs = (pair_m, pair_o, sent_m, sent_o)
    (folded,) = fold(core_row, after(index, one, two), pairs, heads, 0, cut)
    qkv_got, two_got, one_got, folded, *moved = joint((qkv_got, two_got, one_got, folded) + tuple(grad_parts[1:]), ())
    grad_parts = (grad_parts[0],) + tuple(moved)
    qkv_grads = add_rounded(qkv_grads.reshape(shape), qkv_got)
    two = scatter_add(two, two_bits[1], two_got)
    one = scatter_add(one, order[-1], one_got)
    qkv_got = scatter_send(qkv_grads, order[1:2])[1]
    two, two_got = scatter_send(two, two_bits[2:])
    one, one_got = ctx_send(one)
    fold_mine, fold_other = fold(core_row, after(index, one, two, qkv_grads), pairs, heads, cut, block - cut, (folded, small_mid, small_wide, small_end))
    qkv_got, two_got, one_got, fold_mine, fold_other = joint((qkv_got, two_got, one_got, fold_mine, fold_other), ())
    small = fold_mine + swap(fold_other, "tensor")
    qkv_grads = scatter_add(qkv_grads, order[1], qkv_got)
    qkv_grads, qkv_got = scatter_send(qkv_grads, order[2:])
    two = scatter_add(two, two_bits[-1], two_got)
    two, two_got = (two, swap(two, "ctx")) if twice else ctx_send(two)
    groups = joint_groups()
    for group in groups[:-2]:
        small = add_parts(joint_parts(small, group))
    parts = joint_parts(small, groups[-2])
    grad_input = leave_end(grad_parts, clips, counts, core_row, small)
    *parts, grad_input = joint(tuple(parts) + (grad_input,), ())
    small = add_parts(parts)
    parts = joint_parts(small, groups[-1])
    qkv_got, two_got, one_got = joint((qkv_got, two_got, one_got), (small,))
    qkv_grads = scatter_add(qkv_grads, order[-1], qkv_got)
    qkv_grads, qkv_got = ctx_send(qkv_grads)
    one = ctx_add(one, one_got)
    two = flat(ordered(bit_on("ctx", 0) == 1, two, two_got, two.ndim - 2)).astype(F32) if twice else ctx_add(two, two_got)
    qkv_grads = ctx_add(qkv_grads, qkv_got)
    d_gain1, d_shift1, d_bqv, d_bp, d_table, d_gain2, d_shift2, d_b1, d_b2 = unpack(parts, heads)
    rows = w_fc1.shape[0]
    return (
        block_out.reshape(clip_input.shape),
        grad_input.reshape(clip_input.shape),
        d_gain1,
        d_shift1,
        qkv_grads.reshape(rows, 3, half_width).transpose(1, 0, 2),
        d_bqv,
        two[:, :half_width].T,
        d_bp,
        d_table,
        d_gain2,
        d_shift2,
        one,
        d_b1,
        two[:, half_width:].T,
        d_b2,
    )


def solution(mesh):
    in_specs = (
        P("shard", "ctx", None, "tensor"),
        P("shard", "ctx", None, "tensor"),
        P("tensor"),
        P("tensor"),
        P(None, "shard", "tensor"),
        P(None, "tensor"),
        P("tensor", "shard"),
        P("tensor"),
        P("tensor", None),
        P("tensor"),
        P("tensor"),
        P("shard", "tensor"),
        P("tensor"),
        P("tensor", "shard"),
        P("tensor"),
        P(),
        P("ctx", None),
    )
    out_specs = (
        P("shard", "ctx", None, "tensor"),
        P("shard", "ctx", None, "tensor"),
        P("tensor"),
        P("tensor"),
        P(None, "shard", "tensor"),
        P(None, "tensor"),
        P("tensor", "shard"),
        P("tensor"),
        P("tensor", None),
        P("tensor"),
        P("tensor"),
        P("shard", "tensor"),
        P("tensor"),
        P("tensor", "shard"),
        P("tensor"),
    )
    return jax.shard_map(
        on_device, mesh=mesh, in_specs=in_specs, out_specs=out_specs, check_vma=False
    )
```

profile of v0, /device:TPU:0, one launch (start us, length us, event | category | flops | bytes accessed | tf_op | source)
XLA Modules:
  0.0 208.7 jit_solution(14753653980190362356)
XLA Ops:
  0.7 1.1 copy.37
  1.8 4.1 %collective-permute-start = (bf16[1,1,1,64,768]{4,3,2,1,0:T(8,128)(2,1)S(1)}, bf16[1,1,1,64,768]{4,3,2,1,0:T(8,128)(2,1)S(1)}, u32[]{:S(2)}, u32[]{:S(2)}) collective-permute-start(bf16[1,1,1,64,768]{4,3,2,1,0:T(8,128)(2,1)S(1)} %reshape_reshape.3), channel_id=1, source_target_pairs={{0,16},{4,20},{8,24},{12,28},{16,0},{20,4},{24,8},{28,12},{1,17},{... | collective-permute-start | bytes 294920 | tf_op jit(solution)/shard_map/ppermute | solution.py:766
  5.9 1.0 slice.32
  7.1 1.0 pad_maximum_fusion.3
  8.0 1.5 collective-permute-start.2
  9.6 1.7 pack.1.own_ref
  11.3 1.4 copy.38
  12.7 0.8 pad_dynamic-slice_fusion.idx_ref
  13.9 1.6 collective-permute-start.1
  15.5 1.3 collective-permute-done.4.got_ref
  17.5 7.0 %table_lookup.2.rest_0_ = bf16[16,208,512]{2,1,0:T(8,128)(2,1)} custom-call(s32[208,400]{1,0:T(8,128)} %pad_dynamic-slice_fusion.idx_ref, f32[96,256]{1,0:T(8,128)} %pack.1.own_ref, f32[96,256]{1,0:T(8,128)} %copy-done.10), custom_call_target="tpu_custom_call" | custom-call | flops 1 | bytes 1 | tf_op jit(solution)/shard_map/table_lookup/pallas_call | solution.py:177
  24.5 4.6 %collective-permute-done.3 = bf16[1,1,1,64,2304]{4,3,2,1,0:T(8,128)(2,1)S(1)} collective-permute-done((bf16[1,1,1,64,2304]{4,3,2,1,0:T(8,128)(2,1)S(1)}, bf16[1,1,1,64,2304]{4,3,2,1,0:T(8,128)(2,1)S(1)}, u32[]{:S(2)}, u32[]{:S(2)}) %collective-permute-start.3) | collective-permute-done | bytes 294944 | tf_op jit(solution)/shard_map/ppermute | solution.py:766
  29.1 1.9 select_in.1
  31.9 1.6 collective-permute-start.6
  33.4 10.1 %table_lookup.3.own_ref = bf16[16,208,512]{2,1,0:T(8,128)(2,1)} custom-call(s32[208,400]{1,0:T(8,128)} %pad_dynamic-slice_fusion.idx_ref, f32[96,256]{1,0:T(8,128)} %pack.1.own_ref, f32[96,256]{1,0:T(8,128)} %copy-done.10, bf16[16,208,512]{2,1,0:T(8,128)(2,1)} %table_lookup.2.rest_0_), custom_call_target="tpu_custom_call", output_to_operand_aliasing={{}: (3, {})} | custom-call | flops 1 | bytes 1 | tf_op jit(solution)/shard_map/table_lookup/pallas_call | solution.py:177
  43.5 3.5 %collective-permute-done.5 = bf16[2,1,1,64,2304]{4,3,2,1,0:T(8,128)(2,1)S(1)} collective-permute-done((bf16[2,1,1,64,2304]{4,3,2,1,0:T(8,128)(2,1)S(1)}, bf16[2,1,1,64,2304]{4,3,2,1,0:T(8,128)(2,1)S(1)}, u32[]{:S(2)}, u32[]{:S(2)}) %collective-permute-start.5) | collective-permute-done | bytes 589856 | tf_op jit(solution)/shard_map/ppermute | solution.py:766
  47.1 1.2 pad_maximum_fusion
  48.3 1.5 collective-permute-start.8
  50.8 3.5 %collective-permute-done.9.wo_ref = bf16[512,768]{1,0:T(8,128)(2,1)} collective-permute-done((bf16[512,768]{1,0:T(8,128)(2,1)S(1)}, bf16[512,768]{1,0:T(8,128)(2,1)}, u32[]{:S(2)}, u32[]{:S(2)}) %collective-permute-start.9) | collective-permute-done | bytes 786464 | tf_op jit(solution)/shard_map/ppermute | solution.py:766
  54.3 4.9 %front.1 = (bf16[2,512,400]{2,1,0:T(8,128)(2,1)}, bf16[2,512,400]{2,1,0:T(8,128)(2,1)}, bf16[2,512,400]{2,1,0:T(8,128)(2,1)}, bf16[2,512,400]{2,1,0:T(8,128)(2,1)}) custom-call(bf16[2,400,256]{2,1,0:T(8,128)(2,1)} %copy-done.8, bf16[4,400,256]{2,1,0:T(8,128)(2,1)} %copy-done.2, f32[96,256]{1,0:T(8,128)} %pack.1.own_ref, f32[96,256]{1,0:T(8,128)} %copy-done.10, ...), custom_call_target="tpu_custom_call" | custom-call | flops 1 | bytes 1 | tf_op jit(solution)/shard_map/front/pallas_call | solution.py:451
  59.2 15.2 %attend.1 = (bf16[2,512,400]{2,1,0:T(8,128)(2,1)}, f32[2,512,400]{2,1,0:T(8,128)}, f32[2,4,4,400]{3,2,1,0:T(4,128)}) custom-call(s32[1]{0:T(128)} %bitcast.core_ref, bf16[2,512,400]{2,1,0:T(8,128)(2,1)} %get-tuple-element.144.q_ref, bf16[2,512,400]{2,1,0:T(8,128)(2,1)} %get-tuple-element.145.k_ref, bf16[2,512,400]{2,1,0:T(8,128)(2,1)} %get-tuple-element.146.v_ref, ...), custom_call_target="tpu_custom_call" | custom-call | flops 1 | bytes 1 | tf_op jit(solution)/shard_map/attend/pallas_call | solution.py:338
  74.4 2.6 %collective-permute-done.8 = bf16[2,2,1,64,2304]{4,3,2,1,0:T(8,128)(2,1)} collective-permute-done((bf16[2,2,1,64,2304]{4,3,2,1,0:T(8,128)(2,1)}, bf16[2,2,1,64,2304]{4,3,2,1,0:T(8,128)(2,1)}, u32[]{:S(2)}, u32[]{:S(2)}) %collective-permute-start.8) | collective-permute-done | bytes 1179680 | tf_op jit(solution)/shard_map/ppermute | solution.py:766
  77.0 1.3 broadcast_select_fusion.1
  78.4 1.2 broadcast_select_fusion.5
  80.3 1.1 collective-permute-done.11.wo_ref
  81.5 4.6 %middle_forward.1 = (f32[2,400,512]{2,1,0:T(8,128)S(1)}, bf16[2,400,512]{2,1,0:T(8,128)(2,1)S(1)}, bf16[2,400,2048]{2,1,0:T(8,128)(2,1)S(1)}, bf16[2,400,2048]{2,1,0:T(8,128)(2,1)S(1)}) custom-call(bf16[2,400,256]{2,1,0:T(8,128)(2,1)S(1)} %copy-done.9, bf16[4,400,256]{2,1,0:T(8,128)(2,1)S(1)} %copy-done.3, bf16[2,512,400]{2,1,0:T(8,128)(2,1)S(1)} %copy-done.7, ...), custom_call_target="tpu_custom_call" | custom-call | flops 1 | bytes 1 | tf_op jit(solution)/shard_map/middle_forward/pallas_call | solution.py:493
  86.0 16.2 %middle_back.1 = (bf16[2,208,256]{2,1,0:T(8,128)(2,1)}, bf16[2,208,256]{2,1,0:T(8,128)(2,1)}, bf16[2,208,256]{2,1,0:T(8,128)(2,1)}, bf16[2,208,256]{2,1,0:T(8,12...) custom-call(bf16[2,400,256]{2,1,0:T(8,128)(2,1)S(1)} %get-tuple-elem, ...), custom_call_target="tpu_custom_call" | custom-call | flops 1 | bytes 1 | tf_op jit(solution)/shard_map/middle_back/pallas_call | solution.py:586
  103.5 1.2 collective-permute-start.17
  104.7 11.3 %attend_back.2 = (bf16[2,256,400]{2,1,0:T(8,128)(2,1)}, bf16[2,256,400]{2,1,0:T(8,128)(2,1)}, bf16[2,256,400]{2,1,0:T(8,128)(2,1)}, bf16[8,208,512]{2,1,0:T(8,128)(2,1)}, bf16[8,208,512]{2,1,0:T(8,128)(2,1)}) custom-call(s32[1]{0:T(128)} %bitcast.core_ref, bf16[2,512,400]{2,1,0:T(8,128)(2,1)} %get-tuple-element.144.q_ref, ...), custom_call_target="tpu_custom_call" | custom-call | flops 1 | bytes 1 | tf_op jit(solution)/shard_map/attend_back/pallas_call | solution.py:415
  116.1 4.0 %side_grads.1 = bf16[512,768]{1,0:T(8,128)(2,1)} custom-call(bf16[2,512,400]{2,1,0:T(8,128)(2,1)} %get-tuple-element.169.first_ref, bf16[2,256,400]{2,1,0:T(8,128)(2,1)} %get-tuple-element.170.dq_ref.qo_ref, bf16[2,256,400]{2,1,0:T(8,128)(2,1)} %get-tuple-element.171.dk_ref.ko_ref, bf16[2,256,400]{2,1,0:T(8,128)(2,1)} %get-tuple-element.172.dv_ref.vo_ref), custom_call_target="tpu_custom_call" | custom-call | flops 1 | bytes 1 | tf_op jit(solution)/shard_map/side_grads/pallas_call | solution.py:608
  122.7 1.6 collective-permute-start.18
  124.3 11.6 %attend_back.3 = (bf16[2,256,400]{2,1,0:T(8,128)(2,1)}, bf16[2,256,400]{2,1,0:T(8,128)(2,1)}, bf16[2,256,400]{2,1,0:T(8,128)(2,1)}, bf16[8,208,512]{2,1,0:T(8,128)(2,1)}, bf16[8,208,512]{2,1,0:T(8,128)(2,1)}) custom-call(s32[1]{0:T(128)} %bitcast.core_ref, bf16[2,512,400]{2,1,0:T(8,128)(2,1)} %get-tuple-element.144.q_ref, ...), custom_call_target="tpu_custom_call" | custom-call | flops 1 | bytes 1 | tf_op jit(solution)/shard_map/attend_back/pallas_call | solution.py:415
  135.8 1.2 collective-permute-done.18
  137.0 1.2 collective-permute-done.19
  138.4 1.3 add_convert_fusion.2
  139.8 1.6 collective-permute-start.23
  141.6 0.7 constant_dynamic-slice_fusion.6
  142.7 7.8 %back.1 = (bf16[2,208,256]{2,1,0:T(8,128)(2,1)}, bf16[2,208,256]{2,1,0:T(8,128)(2,1)}, bf16[2,208,256]{2,1,0:T(8,128)(2,1)}, bf16[2,208,256]{2,1,0:T(8,128)(2,1)...) custom-call(s32[1]{0:T(128)} %bitcast.18.place_ref, bf16[2,400,256]{2,1,0:T(8,128)(2,1)} %copy-done.8, ...), custom_call_target="tpu_custom_call" | custom-call | flops 1 | bytes 1 | tf_op jit(solution)/shard_map/back/pallas_call | solution.py:661
  151.2 2.2 %select_out.2 = f32[4,392,256]{2,1,0:T(8,128)} custom-call(s32[1]{0:T(128)} %bitcast.core_ref, s32[2,1600,1]{2,1,0:T(8,128)S(1)} %copy-done.4, bf16[416,256]{1,0:T(8,128)(2,1)S(1)} %bitcast.57, bf16[416,256]{1,0:T(8,128)(2,1)S(1)} %collective-permute-done.15.beside_ref, bf16[416,256]{1,0:T(8,128)(2,1)S(1)} %collective-permute-done.16.across_ref, ...), custom_call_target="tpu_custom_call" | custom-call | flops 1 | bytes 1 | tf_op jit(solution)/shard_map/select_out/pallas_call | solution.py:741
  153.4 1.5 collective-permute-start.29
  155.3 1.1 add_convert_fusion.4
  156.4 1.6 collective-permute-start.26
  158.0 1.0 add_convert_fusion.5
  159.1 0.7 copy-done.24
  159.8 8.5 %table_fold.2.init_ref = f32[160,256]{1,0:T(8,128)} custom-call(s32[1]{0:T(128)} %bitcast.core_ref, s32[208,400]{1,0:T(8,128)} %pad_dynamic-slice_fusion.idx_ref, bf16[8,208,512]{2,1,0:T(8,128)(2,1)} %get-tuple-element.198.pair_m, bf16[8,208,512]{2,1,0:T(8,128)(2,1)} %get-tuple-element.199.pair_o, bf16[8,208,512]{2,1,0:T(8,128)(2,1)} %collective-permute-done.24.sent_m, ...), custom_call_target="tpu_custom_call" | custom-call | flops 1 | bytes 1 | tf_op jit(solution)/shard_map/table_fold/pallas_call | solution.py:252
  169.5 1.1 fusion
  170.6 1.4 collective-permute-start.31
  172.7 2.6 %collective-permute-start.32 = (bf16[1,1,1,32,1280]{4,3,2,1,0:T(8,128)(2,1)}, bf16[1,1,1,32,1280]{4,3,2,1,0:T(8,128)(2,1)}, u32[]{:S(2)}, u32[]{:S(2)}) collective-permute-start(bf16[1,1,1,32,1280]{4,3,2,1,0:T(8,128)(2,1)} %constant_dynamic-slice_fusion.1), channel_id=1, source_target_pairs={{0,16},{4,20},{8,24},{12,28},{16,0},{20,4},{24,8},{28,12},{1,17},{... | collective-permute-start | bytes 245768 | tf_op jit(solution)/shard_map/ppermute | solution.py:766
  175.2 9.8 %table_fold.3 = (f32[96,256]{1,0:T(8,128)}, f32[96,256]{1,0:T(8,128)}) custom-call(s32[1]{0:T(128)} %bitcast.core_ref, s32[208,400]{1,0:T(8,128)} %pad_dynamic-slice_fusion.idx_ref, bf16[8,208,512]{2,1,0:T(8,128)(2,1)} %get-tuple-element.198.pair_m, bf16[8,208,512]{2,1,0:T(8,128)(2,1)} %get-tuple-element.199.pair_o, ...), custom_call_target="tpu_custom_call" | custom-call | flops 1 | bytes 1 | tf_op jit(solution)/shard_map/table_fold/pallas_call | solution.py:252
  185.1 1.0 add_convert_fusion.10
  186.7 1.5 collective-permute-done.34
  188.2 0.9 add.160
  189.1 1.6 collective-permute-start.35
  190.6 1.5 collective-permute-start.36
  192.6 1.3 collective-permute-start.41
  194.0 2.2 %select_out.3 = f32[4,392,256]{2,1,0:T(8,128)} custom-call(s32[1]{0:T(128)} %bitcast.core_ref, s32[2,1600,1]{2,1,0:T(8,128)S(1)} %copy-done.4, bf16[416,256]{1,0:T(8,128)(2,1)S(1)} %bitcast.58, bf16[416,256]{1,0:T(8,128)(2,1)S(1)} %collective-permute-done.28.beside_ref, bf16[416,256]{1,0:T(8,128)(2,1)S(1)} %collective-permute-done.29.across_ref, ...), custom_call_target="tpu_custom_call" | custom-call | flops 1 | bytes 1 | tf_op jit(solution)/shard_map/select_out/pallas_call | solution.py:741
  196.2 0.9 collective-permute-done.37
  197.8 1.8 collective-permute-start.39
  199.5 2.1 %collective-permute-start.40 = (bf16[96,256]{1,0:T(8,128)(2,1)S(1)}, bf16[96,256]{1,0:T(8,128)(2,1)S(1)}, u32[]{:S(2)}, u32[]{:S(2)}) collective-permute-start(bf16[96,256]{1,0:T(8,128)(2,1)S(1)} %add_add_fusion.a_ref), channel_id=1, source_target_pairs={{0,24},{2,26},{4,28},{6,30},{8,16},{10,18},{12,20},{14,22},{16,8},... | collective-permute-start | bytes 147464 | tf_op jit(solution)/shard_map/ppermute | solution.py:864
  201.6 0.7 convert_add_fusion.1
  202.4 0.7 slice_bitcast_fusion
  204.4 1.0 collective-permute-done.40.d_ref
  206.1 1.5 unpack.1
  208.0 0.7 copy.41
  (171 shorter events, 15.5 us)
Async XLA Ops:
  0.6 49.6 %copy-start = (s32[4,392]{1,0:T(4,128)S(1)}, s32[4,392]{1,0:T(4,128)}, u32[]{:S(2)}) copy-start(s32[4,392]{1,0:T(4,128)} %param.36) | copy-start | bytes 18820
  0.7 6.4 %copy-start.13 = (bf16[1,4,392,256]{3,2,1,0:T(8,128)(2,1)S(1)}, bf16[1,4,392,256]{3,2,1,0:T(8,128)(2,1)}, u32[]{:S(2)}) copy-start(bf16[1,4,392,256]{3,2,1,0:T(8,128)(2,1)} %param.21) | copy-start | bytes 2408452
  1.8 11.6 %collective-permute-start = (bf16[1,1,1,64,768]{4,3,2,1,0:T(8,128)(2,1)S(1)}, bf16[1,1,1,64,768]{4,3,2,1,0:T(8,128)(2,1)S(1)}, u32[]{:S(2)}, u32[]{:S(2)}) collective-permute-start(bf16[1,1,1,64,768]{4,3,2,1,0:T(8,128)(2,1)S(1)} %reshape_reshape.3), channel_id=1, source_target_pairs={{0,16},{4,20},{8,24},{12,28},{16,0},{20,4},{24,8},{28,12},{1,17},{... | collective-permute-start | bytes 294920 | tf_op jit(solution)/shard_map/ppermute | solution.py:766
  7.0 2.6 %copy-start.30 = (bf16[1024,64]{0,1:T(8,128)(2,1)S(1)}, bf16[1024,64]{0,1:T(8,128)(2,1)}, u32[]{:S(2)}) copy-start(bf16[1024,64]{0,1:T(8,128)(2,1)} %param.33) | copy-start | bytes 393220
  8.0 21.0 %collective-permute-start.2 = (bf16[1600,256]{1,0:T(8,128)(2,1)}, bf16[1600,256]{1,0:T(8,128)(2,1)S(1)}, u32[]{:S(2)}, u32[]{:S(2)}) collective-permute-start(bf16[1600,256]{1,0:T(8,128)(2,1)} %bitcast.5), channel_id=1, source_target_pairs={{0,2},{2,0},{1,3},{3,1},{4,6},{6,4},{5,7},{7,5},{8,10},{10,8},{9,1... | collective-permute-start | bytes 2457608 | tf_op jit(solution)/shard_map/ppermute | solution.py:766
  12.7 2.8 %copy-start.5 = (f32[96,256]{1,0:T(8,128)S(1)}, f32[96,256]{1,0:T(8,128)}, u32[]{:S(2)}) copy-start(f32[96,256]{1,0:T(8,128)} %pack.1.own_ref) | copy-start | bytes 294916
  13.5 15.5 %collective-permute-start.3 = (bf16[1,1,1,64,2304]{4,3,2,1,0:T(8,128)(2,1)S(1)}, bf16[1,1,1,64,2304]{4,3,2,1,0:T(8,128)(2,1)S(1)}, u32[]{:S(2)}, u32[]{:S(2)}) collective-permute-start(bf16[1,1,1,64,2304]{4,3,2,1,0:T(8,128)(2,1)S(1)} %maximum_bitcast_fusion), channel_id=1, source_target_pairs={{0,16},{4,20},{8,24},{12,28},{16,0},{20,4},{24,8},{28,12},{1,17},{... | collective-permute-start | bytes 884744 | tf_op jit(solution)/shard_map/ppermute | solution.py:766
  13.9 10.5 %collective-permute-start.1 = (bf16[2,1,1,64,768]{4,3,2,1,0:T(8,128)(2,1)S(1)}, bf16[2,1,1,64,768]{4,3,2,1,0:T(8,128)(2,1)S(1)}, u32[]{:S(2)}, u32[]{:S(2)}) collective-permute-start(bf16[2,1,1,64,768]{4,3,2,1,0:T(8,128)(2,1)S(1)} %pad_maximum_fusion.7), channel_id=1, source_target_pairs={{0,8},{4,12},{8,0},{12,4},{16,24},{20,28},{24,16},{28,20},{1,9},{5... | collective-permute-start | bytes 589832 | tf_op jit(solution)/shard_map/ppermute | solution.py:766
  15.5 1.3 collective-permute-start.4
  17.5 11.7 %copy-start.14 = (s32[2,1632,1]{2,1,0:T(8,128)S(1)}, s32[2,1632,1]{2,1,0:T(8,128)}, u32[]{:S(2)}) copy-start(s32[2,1632,1]{2,1,0:T(8,128)} %constant.103.clone.picks_ref) | copy-start | bytes 39172
  24.5 4.6 %copy-start.12 = (bf16[1,4,392,256]{3,2,1,0:T(8,128)(2,1)S(1)}, bf16[1,4,392,256]{3,2,1,0:T(8,128)(2,1)}, u32[]{:S(2)}) copy-start(bf16[1,4,392,256]{3,2,1,0:T(8,128)(2,1)} %param.20) | copy-start | bytes 2408452
  31.1 15.9 %collective-permute-start.7 = (bf16[4,400,256]{2,1,0:T(8,128)(2,1)S(1)}, bf16[4,400,256]{2,1,0:T(8,128)(2,1)S(1)}, u32[]{:S(2)}, u32[]{:S(2)}) collective-permute-start(bf16[4,400,256]{2,1,0:T(8,128)(2,1)S(1)} %get-tuple-element.137), channel_id=1, source_target_pairs={{0,1},{1,0},{2,3},{3,2},{4,5},{5,4},{6,7},{7,6},{8,9},{9,8},{10,11... | collective-permute-start | bytes 2457608 | tf_op jit(solution)/shard_map/ppermute | solution.py:766
  31.2 15.8 %collective-permute-start.5 = (bf16[2,1,1,64,2304]{4,3,2,1,0:T(8,128)(2,1)S(1)}, bf16[2,1,1,64,2304]{4,3,2,1,0:T(8,128)(2,1)S(1)}, u32[]{:S(2)}, u32[]{:S(2)}) collective-permute-start(bf16[2,1,1,64,2304]{4,3,2,1,0:T(8,128)(2,1)S(1)} %pad_maximum_fusion.5), channel_id=1, source_target_pairs={{0,8},{4,12},{8,0},{12,4},{16,24},{20,28},{24,16},{28,20},{1,9},{5... | collective-permute-start | bytes 1769480 | tf_op jit(solution)/shard_map/ppermute | solution.py:766
  31.9 11.6 %collective-permute-start.6 = (bf16[2,2,1,64,768]{4,3,2,1,0:T(8,128)(2,1)S(1)}, bf16[2,2,1,64,768]{4,3,2,1,0:T(8,128)(2,1)S(1)}, u32[]{:S(2)}, u32[]{:S(2)}) collective-permute-start(bf16[2,2,1,64,768]{4,3,2,1,0:T(8,128)(2,1)S(1)} %pad_maximum_fusion.6), channel_id=1, source_target_pairs={{0,4},{4,0},{8,12},{12,8},{16,20},{20,16},{24,28},{28,24},{1,5},{5... | collective-permute-start | bytes 1179656 | tf_op jit(solution)/shard_map/ppermute | solution.py:766
  47.0 12.2 %collective-permute-start.10 = (bf16[16,208,512]{2,1,0:T(8,128)(2,1)}, bf16[16,208,512]{2,1,0:T(8,128)(2,1)}, u32[]{:S(2)}, u32[]{:S(2)}) collective-permute-start(bf16[16,208,512]{2,1,0:T(8,128)(2,1)} %table_lookup.3.own_ref), channel_id=1, source_target_pairs={{0,1},{1,0},{2,3},{3,2},{4,5},{5,4},{6,7},{7,6},{8,9},{9,8},{10,11... | collective-permute-start | bytes 10223624 | tf_op jit(solution)/shard_map/ppermute | solution.py:766
  48.3 28.6 %collective-permute-start.8 = (bf16[2,2,1,64,2304]{4,3,2,1,0:T(8,128)(2,1)}, bf16[2,2,1,64,2304]{4,3,2,1,0:T(8,128)(2,1)}, u32[]{:S(2)}, u32[]{:S(2)}) collective-permute-start(bf16[2,2,1,64,2304]{4,3,2,1,0:T(8,128)(2,1)} %pad_maximum_fusion), channel_id=1, source_target_pairs={{0,4},{4,0},{8,12},{12,8},{16,20},{20,16},{24,28},{28,24},{1,5},{5... | collective-permute-start | bytes 3538952 | tf_op jit(solution)/shard_map/ppermute | solution.py:766
  50.0 4.4 %copy-start.17 = (bf16[2,2,2,64,768]{4,3,2,1,0:T(8,128)(2,1)}, bf16[2,2,2,64,768]{4,3,2,1,0:T(8,128)(2,1)S(1)}, u32[]{:S(2)}) copy-start(bf16[2,2,2,64,768]{4,3,2,1,0:T(8,128)(2,1)S(1)} %pad_maximum_fusion.4) | copy-start | bytes 2359300
  50.0 4.4 %collective-permute-start.9 = (bf16[512,768]{1,0:T(8,128)(2,1)S(1)}, bf16[512,768]{1,0:T(8,128)(2,1)}, u32[]{:S(2)}, u32[]{:S(2)}) collective-permute-start(bf16[512,768]{1,0:T(8,128)(2,1)S(1)} %bitcast.59), channel_id=1, source_target_pairs={{0,1},{1,0},{2,3},{3,2},{4,5},{5,4},{6,7},{7,6},{8,9},{9,8},{10,11... | collective-permute-start | bytes 2359304 | tf_op jit(solution)/shard_map/ppermute | solution.py:766
  78.3 3.1 %collective-permute-start.11 = (bf16[512,1280]{1,0:T(8,128)(2,1)S(1)}, bf16[512,1280]{1,0:T(8,128)(2,1)S(1)}, u32[]{:S(2)}, u32[]{:S(2)}) collective-permute-start(bf16[512,1280]{1,0:T(8,128)(2,1)S(1)} %bitcast.48), channel_id=1, source_target_pairs={{0,1},{1,0},{2,3},{3,2},{4,5},{5,4},{6,7},{7,6},{8,9},{9,8},{10,11... | collective-permute-start | bytes 3932168 | tf_op jit(solution)/shard_map/ppermute | solution.py:766
  78.4 3.0 %copy-start.9 = (bf16[2,400,256]{2,1,0:T(8,128)(2,1)S(1)}, bf16[2,400,256]{2,1,0:T(8,128)(2,1)}, u32[]{:S(2)}) copy-start(bf16[2,400,256]{2,1,0:T(8,128)(2,1)} %copy-done.8) | copy-start | bytes 1228804
  79.8 6.3 %collective-permute-start.12 = (bf16[512,1024]{1,0:T(8,128)(2,1)S(1)}, bf16[512,1024]{1,0:T(8,128)(2,1)S(1)}, u32[]{:S(2)}, u32[]{:S(2)}) collective-permute-start(bf16[512,1024]{1,0:T(8,128)(2,1)S(1)} %bitcast.51), channel_id=1, source_target_pairs={{0,1},{1,0},{2,3},{3,2},{4,5},{5,4},{6,7},{7,6},{8,9},{9,8},{10,11... | collective-permute-start | bytes 3145736 | tf_op jit(solution)/shard_map/ppermute | solution.py:766
  102.3 13.8 %collective-permute-start.14 = (bf16[512,1280]{1,0:T(8,128)(2,1)}, bf16[512,1280]{1,0:T(8,128)(2,1)S(1)}, u32[]{:S(2)}, u32[]{:S(2)}) collective-permute-start(bf16[512,1280]{1,0:T(8,128)(2,1)} %get-tuple-element.157), channel_id=1, source_target_pairs={{0,1},{1,0},{2,3},{3,2},{4,5},{5,4},{6,7},{7,6},{8,9},{9,8},{10,11... | collective-permute-start | bytes 3932168 | tf_op jit(solution)/shard_map/ppermute | solution.py:766
  102.5 13.6 %collective-permute-start.13 = (bf16[512,1024]{1,0:T(8,128)(2,1)}, bf16[512,1024]{1,0:T(8,128)(2,1)S(1)}, u32[]{:S(2)}, u32[]{:S(2)}) collective-permute-start(bf16[512,1024]{1,0:T(8,128)(2,1)} %get-tuple-element.156), channel_id=1, source_target_pairs={{0,1},{1,0},{2,3},{3,2},{4,5},{5,4},{6,7},{7,6},{8,9},{9,8},{10,11... | collective-permute-start | bytes 3145736 | tf_op jit(solution)/shard_map/ppermute | solution.py:766
  102.9 13.2 %collective-permute-start.15 = (bf16[416,256]{1,0:T(8,128)(2,1)}, bf16[416,256]{1,0:T(8,128)(2,1)S(1)}, u32[]{:S(2)}, u32[]{:S(2)}) collective-permute-start(bf16[416,256]{1,0:T(8,128)(2,1)} %bitcast.77), channel_id=1, source_target_pairs={{0,1},{1,0},{2,3},{3,2},{4,5},{5,4},{6,7},{7,6},{8,9},{9,8},{10,11... | collective-permute-start | bytes 638984 | tf_op jit(solution)/shard_map/ppermute | solution.py:766
  103.0 13.0 %collective-permute-start.16 = (bf16[416,256]{1,0:T(8,128)(2,1)}, bf16[416,256]{1,0:T(8,128)(2,1)S(1)}, u32[]{:S(2)}, u32[]{:S(2)}) collective-permute-start(bf16[416,256]{1,0:T(8,128)(2,1)} %bitcast.76), channel_id=1, source_target_pairs={{0,2},{2,0},{1,3},{3,1},{4,6},{6,4},{5,7},{7,5},{8,10},{10,8},{9,1... | collective-permute-start | bytes 638984 | tf_op jit(solution)/shard_map/ppermute | solution.py:766
  103.5 12.6 %collective-permute-start.17 = (bf16[416,256]{1,0:T(8,128)(2,1)}, bf16[416,256]{1,0:T(8,128)(2,1)S(1)}, u32[]{:S(2)}, u32[]{:S(2)}) collective-permute-start(bf16[416,256]{1,0:T(8,128)(2,1)} %bitcast.75), channel_id=1, source_target_pairs={{0,3},{1,2},{2,1},{3,0},{4,7},{5,6},{6,5},{7,4},{8,11},{9,10},{10,... | collective-permute-start | bytes 638984 | tf_op jit(solution)/shard_map/ppermute | solution.py:978
  116.1 4.0 %copy-start.22 = (bf16[512,1024]{1,0:T(8,128)(2,1)}, bf16[512,1024]{1,0:T(8,128)(2,1)S(1)}, u32[]{:S(2)}) copy-start(bf16[512,1024]{1,0:T(8,128)(2,1)S(1)} %collective-permute-done.13) | copy-start | bytes 3145732
  116.1 4.4 %copy-start.36 = (bf16[8,208,512]{2,1,0:T(8,128)(2,1)S(1)}, bf16[8,208,512]{2,1,0:T(8,128)(2,1)}, u32[]{:S(2)}) copy-start(bf16[8,208,512]{2,1,0:T(8,128)(2,1)} %get-tuple-element.173) | copy-start | bytes 5111812
  116.1 4.5 %copy-start.20 = (bf16[512,1280]{1,0:T(8,128)(2,1)S(1)}, bf16[512,1280]{1,0:T(8,128)(2,1)}, u32[]{:S(2)}) copy-start(bf16[512,1280]{1,0:T(8,128)(2,1)} %get-tuple-element.167) | copy-start | bytes 3932164
  120.1 18.2 %collective-permute-start.20 = (bf16[512,768]{1,0:T(8,128)(2,1)}, bf16[512,768]{1,0:T(8,128)(2,1)}, u32[]{:S(2)}, u32[]{:S(2)}) collective-permute-start(bf16[512,768]{1,0:T(8,128)(2,1)} %side_grads.1), channel_id=1, source_target_pairs={{0,1},{1,0},{2,3},{3,2},{4,5},{5,4},{6,7},{7,6},{8,9},{9,8},{10,11... | collective-permute-start | bytes 2359304 | tf_op jit(solution)/shard_map/ppermute | solution.py:766
  120.5 17.7 %collective-permute-start.21 = (bf16[8,208,512]{2,1,0:T(8,128)(2,1)S(1)}, bf16[8,208,512]{2,1,0:T(8,128)(2,1)}, u32[]{:S(2)}, u32[]{:S(2)}) collective-permute-start(bf16[8,208,512]{2,1,0:T(8,128)(2,1)S(1)} %copy-done.36), channel_id=1, source_target_pairs={{0,1},{1,0},{2,3},{3,2},{4,5},{5,4},{6,7},{7,6},{8,9},{9,8},{10,11... | collective-permute-start | bytes 5111816 | tf_op jit(solution)/shard_map/ppermute | solution.py:766
  121.0 17.2 %collective-permute-start.19 = (bf16[2,2,2,32,1280]{4,3,2,1,0:T(8,128)(2,1)S(1)}, bf16[2,2,2,32,1280]{4,3,2,1,0:T(8,128)(2,1)}, u32[]{:S(2)}, u32[]{:S(2)}) collective-permute-start(bf16[2,2,2,32,1280]{4,3,2,1,0:T(8,128)(2,1)S(1)} %constant_dynamic-slice_fusion.7), channel_id=1, source_target_pairs={{0,2},{2,0},{1,3},{3,1},{4,6},{6,4},{5,7},{7,5},{8,10},{10,8},{9,1... | collective-permute-start | bytes 1966088 | tf_op jit(solution)/shard_map/ppermute | solution.py:766
  122.7 14.3 %collective-permute-start.18 = (bf16[2,2,1,64,1024]{4,3,2,1,0:T(8,128)(2,1)S(1)}, bf16[2,2,1,64,1024]{4,3,2,1,0:T(8,128)(2,1)S(1)}, u32[]{:S(2)}, u32[]{:S(2)}) collective-permute-start(bf16[2,2,1,64,1024]{4,3,2,1,0:T(8,128)(2,1)S(1)} %constant_dynamic-slice_fusion.8), channel_id=1, source_target_pairs={{0,4},{4,0},{8,12},{12,8},{16,20},{20,16},{24,28},{28,24},{1,5},{5... | collective-permute-start | bytes 1572872 | tf_op jit(solution)/shard_map/ppermute | solution.py:766
  138.3 17.0 %collective-permute-start.24 = (bf16[8,208,512]{2,1,0:T(8,128)(2,1)}, bf16[8,208,512]{2,1,0:T(8,128)(2,1)}, u32[]{:S(2)}, u32[]{:S(2)}) collective-permute-start(bf16[8,208,512]{2,1,0:T(8,128)(2,1)} %get-tuple-element.179), channel_id=1, source_target_pairs={{0,1},{1,0},{2,3},{3,2},{4,5},{5,4},{6,7},{7,6},{8,9},{9,8},{10,11... | collective-permute-start | bytes 5111816 | tf_op jit(solution)/shard_map/ppermute | solution.py:766
  138.4 3.0 %copy-start.27 = (bf16[2,2,1,64,1024]{4,3,2,1,0:T(8,128)(2,1)S(1)}, bf16[2,2,1,64,1024]{4,3,2,1,0:T(8,128)(2,1)}, u32[]{:S(2)}) copy-start(bf16[2,2,1,64,1024]{4,3,2,1,0:T(8,128)(2,1)} %copy-done.26) | copy-start | bytes 1572868
  139.8 15.1 %collective-permute-start.23 = (bf16[2,2,1,32,1280]{4,3,2,1,0:T(8,128)(2,1)S(1)}, bf16[2,2,1,32,1280]{4,3,2,1,0:T(8,128)(2,1)}, u32[]{:S(2)}, u32[]{:S(2)}) collective-permute-start(bf16[2,2,1,32,1280]{4,3,2,1,0:T(8,128)(2,1)S(1)} %constant_dynamic-slice_fusion.5), channel_id=1, source_target_pairs={{0,4},{4,0},{8,12},{12,8},{16,20},{20,16},{24,28},{28,24},{1,5},{5... | collective-permute-start | bytes 983048 | tf_op jit(solution)/shard_map/ppermute | solution.py:766
  142.3 11.1 %collective-permute-start.22 = (bf16[2,1,1,64,1024]{4,3,2,1,0:T(8,128)(2,1)}, bf16[2,1,1,64,1024]{4,3,2,1,0:T(8,128)(2,1)}, u32[]{:S(2)}, u32[]{:S(2)}) collective-permute-start(bf16[2,1,1,64,1024]{4,3,2,1,0:T(8,128)(2,1)} %constant_dynamic-slice_fusion.6), channel_id=1, source_target_pairs={{0,8},{4,12},{8,0},{12,4},{16,24},{20,28},{24,16},{28,20},{1,9},{5... | collective-permute-start | bytes 786440 | tf_op jit(solution)/shard_map/ppermute | solution.py:766
  142.7 8.4 %copy-start.4 = (s32[2,1600,1]{2,1,0:T(8,128)S(1)}, s32[2,1600,1]{2,1,0:T(8,128)}, u32[]{:S(2)}) copy-start(s32[2,1600,1]{2,1,0:T(8,128)} %constant.104.clone.picks_ref) | copy-start | bytes 38404
  142.7 8.4 %copy-start.15 = (bf16[2,208,256]{2,1,0:T(8,128)(2,1)S(1)}, bf16[2,208,256]{2,1,0:T(8,128)(2,1)}, u32[]{:S(2)}) copy-start(bf16[2,208,256]{2,1,0:T(8,128)(2,1)} %get-tuple-element.180) | copy-start | bytes 638980
  150.5 17.7 %collective-permute-start.25 = (bf16[2,2,1,64,768]{4,3,2,1,0:T(8,128)(2,1)}, bf16[2,2,1,64,768]{4,3,2,1,0:T(8,128)(2,1)}, u32[]{:S(2)}, u32[]{:S(2)}) collective-permute-start(bf16[2,2,1,64,768]{4,3,2,1,0:T(8,128)(2,1)} %bitcast.74), channel_id=1, source_target_pairs={{0,4},{4,0},{8,12},{12,8},{16,20},{20,16},{24,28},{28,24},{1,5},{5... | collective-permute-start | bytes 1179656 | tf_op jit(solution)/shard_map/ppermute | solution.py:766
  151.2 4.1 %copy-start.19 = (bf16[2,2,2,32,1280]{4,3,2,1,0:T(8,128)(2,1)S(1)}, bf16[2,2,2,32,1280]{4,3,2,1,0:T(8,128)(2,1)}, u32[]{:S(2)}) copy-start(bf16[2,2,2,32,1280]{4,3,2,1,0:T(8,128)(2,1)} %copy-done.18) | copy-start | bytes 1966084
  151.2 7.9 %collective-permute-start.28 = (bf16[416,256]{1,0:T(8,128)(2,1)}, bf16[416,256]{1,0:T(8,128)(2,1)S(1)}, u32[]{:S(2)}, u32[]{:S(2)}) collective-permute-start(bf16[416,256]{1,0:T(8,128)(2,1)} %bitcast.78), channel_id=1, source_target_pairs={{0,1},{1,0},{2,3},{3,2},{4,5},{5,4},{6,7},{7,6},{8,9},{9,8},{10,11... | collective-permute-start | bytes 638984 | tf_op jit(solution)/shard_map/ppermute | solution.py:766
  153.4 14.9 %collective-permute-start.29 = (bf16[416,256]{1,0:T(8,128)(2,1)}, bf16[416,256]{1,0:T(8,128)(2,1)S(1)}, u32[]{:S(2)}, u32[]{:S(2)}) collective-permute-start(bf16[416,256]{1,0:T(8,128)(2,1)} %bitcast.25), channel_id=1, source_target_pairs={{0,2},{2,0},{1,3},{3,1},{4,6},{6,4},{5,7},{7,5},{8,10},{10,8},{9,1... | collective-permute-start | bytes 638984 | tf_op jit(solution)/shard_map/ppermute | solution.py:766
  154.9 13.4 %collective-permute-start.30 = (bf16[416,256]{1,0:T(8,128)(2,1)}, bf16[416,256]{1,0:T(8,128)(2,1)S(1)}, u32[]{:S(2)}, u32[]{:S(2)}) collective-permute-start(bf16[416,256]{1,0:T(8,128)(2,1)} %bitcast.26), channel_id=1, source_target_pairs={{0,3},{1,2},{2,1},{3,0},{4,7},{5,6},{6,5},{7,4},{8,11},{9,10},{10,... | collective-permute-start | bytes 638984 | tf_op jit(solution)/shard_map/ppermute | solution.py:978
  156.4 12.5 %collective-permute-start.26 = (bf16[2,1,1,32,1280]{4,3,2,1,0:T(8,128)(2,1)S(1)}, bf16[2,1,1,32,1280]{4,3,2,1,0:T(8,128)(2,1)S(1)}, u32[]{:S(2)}, u32[]{:S(2)}) collective-permute-start(bf16[2,1,1,32,1280]{4,3,2,1,0:T(8,128)(2,1)S(1)} %constant_dynamic-slice_fusion.4), channel_id=1, source_target_pairs={{0,8},{4,12},{8,0},{12,4},{16,24},{20,28},{24,16},{28,20},{1,9},{5... | collective-permute-start | bytes 491528 | tf_op jit(solution)/shard_map/ppermute | solution.py:766
  159.7 9.1 %collective-permute-start.27 = (bf16[1,1,1,64,1024]{4,3,2,1,0:T(8,128)(2,1)S(1)}, bf16[1,1,1,64,1024]{4,3,2,1,0:T(8,128)(2,1)S(1)}, u32[]{:S(2)}, u32[]{:S(2)}) collective-permute-start(bf16[1,1,1,64,1024]{4,3,2,1,0:T(8,128)(2,1)S(1)} %constant_dynamic-slice_fusion.3), channel_id=1, source_target_pairs={{0,16},{4,20},{8,24},{12,28},{16,0},{20,4},{24,8},{28,12},{1,17},{... | collective-permute-start | bytes 393224 | tf_op jit(solution)/shard_map/ppermute | solution.py:766
  159.7 9.2 %copy-start.25 = (bf16[2,1,1,64,1024]{4,3,2,1,0:T(8,128)(2,1)S(1)}, bf16[2,1,1,64,1024]{4,3,2,1,0:T(8,128)(2,1)}, u32[]{:S(2)}) copy-start(bf16[2,1,1,64,1024]{4,3,2,1,0:T(8,128)(2,1)} %copy-done.24) | copy-start | bytes 786436
  159.7 9.8 %copy-start.28 = (bf16[4,64,768]{2,1,0:T(8,128)(2,1)S(1)}, bf16[4,64,768]{2,1,0:T(8,128)(2,1)}, u32[]{:S(2)}) copy-start(bf16[4,64,768]{2,1,0:T(8,128)(2,1)} %get-tuple-element.193) | copy-start | bytes 1179652
  169.0 16.1 %collective-permute-start.33 = (bf16[64,1024]{1,0:T(8,128)(2,1)S(1)}, bf16[64,1024]{1,0:T(8,128)(2,1)S(1)}, u32[]{:S(2)}, u32[]{:S(2)}) collective-permute-start(bf16[64,1024]{1,0:T(8,128)(2,1)S(1)} %fusion.4), channel_id=1, source_target_pairs={{0,2},{2,0},{1,3},{3,1},{4,6},{6,4},{5,7},{7,5},{8,10},{10,8},{9,1... | collective-permute-start | bytes 393224 | tf_op jit(solution)/shard_map/ppermute | solution.py:766
  170.6 14.4 %collective-permute-start.31 = (bf16[2,1,1,64,768]{4,3,2,1,0:T(8,128)(2,1)S(1)}, bf16[2,1,1,64,768]{4,3,2,1,0:T(8,128)(2,1)S(1)}, u32[]{:S(2)}, u32[]{:S(2)}) collective-permute-start(bf16[2,1,1,64,768]{4,3,2,1,0:T(8,128)(2,1)S(1)} %constant_dynamic-slice_fusion.2), channel_id=1, source_target_pairs={{0,8},{4,12},{8,0},{12,4},{16,24},{20,28},{24,16},{28,20},{1,9},{5... | collective-permute-start | bytes 589832 | tf_op jit(solution)/shard_map/ppermute | solution.py:766
  172.7 12.4 %collective-permute-start.32 = (bf16[1,1,1,32,1280]{4,3,2,1,0:T(8,128)(2,1)}, bf16[1,1,1,32,1280]{4,3,2,1,0:T(8,128)(2,1)}, u32[]{:S(2)}, u32[]{:S(2)}) collective-permute-start(bf16[1,1,1,32,1280]{4,3,2,1,0:T(8,128)(2,1)} %constant_dynamic-slice_fusion.1), channel_id=1, source_target_pairs={{0,16},{4,20},{8,24},{12,28},{16,0},{20,4},{24,8},{28,12},{1,17},{... | collective-permute-start | bytes 245768 | tf_op jit(solution)/shard_map/ppermute | solution.py:766
  185.1 8.9 %copy-start.16 = (bf16[2,208,256]{2,1,0:T(8,128)(2,1)S(1)}, bf16[2,208,256]{2,1,0:T(8,128)(2,1)}, u32[]{:S(2)}) copy-start(bf16[2,208,256]{2,1,0:T(8,128)(2,1)} %get-tuple-element.216) | copy-start | bytes 638980
  186.1 15.6 %collective-permute-start.42 = (bf16[1,1,1,32,1280]{4,3,2,1,0:T(8,128)(2,1)S(1)}, bf16[1,1,1,32,1280]{4,3,2,1,0:T(8,128)(2,1)S(1)}, u32[]{:S(2)}, u32[]{:S(2)}) collective-permute-start(bf16[1,1,1,32,1280]{4,3,2,1,0:T(8,128)(2,1)S(1)} %add_convert_fusion.10), channel_id=1, source_target_pairs={{0,2},{2,0},{1,3},{3,1},{4,6},{6,4},{5,7},{7,5},{8,10},{10,8},{9,1... | collective-permute-start | bytes 245768 | tf_op jit(solution)/shard_map/ppermute | solution.py:766
  186.7 1.5 collective-permute-start.34
  189.1 7.1 %collective-permute-start.35 = (bf16[96,256]{1,0:T(8,128)(2,1)S(1)}, bf16[96,256]{1,0:T(8,128)(2,1)S(1)}, u32[]{:S(2)}, u32[]{:S(2)}) collective-permute-start(bf16[96,256]{1,0:T(8,128)(2,1)S(1)} %add.160), channel_id=1, source_target_pairs={{0,2},{2,0},{4,6},{6,4},{8,10},{10,8},{12,14},{14,12},{16,18},{18,... | collective-permute-start | bytes 147464 | tf_op jit(solution)/shard_map/ppermute | solution.py:864
  190.6 5.6 %collective-permute-start.36 = (bf16[96,256]{1,0:T(8,128)(2,1)S(1)}, bf16[96,256]{1,0:T(8,128)(2,1)S(1)}, u32[]{:S(2)}, u32[]{:S(2)}) collective-permute-start(bf16[96,256]{1,0:T(8,128)(2,1)S(1)} %add.160), channel_id=1, source_target_pairs={{0,4},{2,6},{4,0},{6,2},{8,12},{10,14},{12,8},{14,10},{16,20},{18,... | collective-permute-start | bytes 147464 | tf_op jit(solution)/shard_map/ppermute | solution.py:864
  192.2 5.0 %collective-permute-start.37 = (bf16[96,256]{1,0:T(8,128)(2,1)S(1)}, bf16[96,256]{1,0:T(8,128)(2,1)S(1)}, u32[]{:S(2)}, u32[]{:S(2)}) collective-permute-start(bf16[96,256]{1,0:T(8,128)(2,1)S(1)} %add.160), channel_id=1, source_target_pairs={{0,6},{2,4},{4,2},{6,0},{8,14},{10,12},{12,10},{14,8},{16,22},{18,... | collective-permute-start | bytes 147464 | tf_op jit(solution)/shard_map/ppermute | solution.py:864
  192.6 9.0 %collective-permute-start.41 = (bf16[1,1,1,64,768]{4,3,2,1,0:T(8,128)(2,1)S(1)}, bf16[1,1,1,64,768]{4,3,2,1,0:T(8,128)(2,1)S(1)}, u32[]{:S(2)}, u32[]{:S(2)}) collective-permute-start(bf16[1,1,1,64,768]{4,3,2,1,0:T(8,128)(2,1)S(1)} %constant_dynamic-slice_fusion), channel_id=1, source_target_pairs={{0,16},{4,20},{8,24},{12,28},{16,0},{20,4},{24,8},{28,12},{1,17},{... | collective-permute-start | bytes 294920 | tf_op jit(solution)/shard_map/ppermute | solution.py:766
  197.2 8.3 %copy-start.29 = (bf16[96,256]{1,0:T(8,128)(2,1)}, bf16[96,256]{1,0:T(8,128)(2,1)S(1)}, u32[]{:S(2)}) copy-start(bf16[96,256]{1,0:T(8,128)(2,1)S(1)} %add_add_fusion.a_ref) | copy-start | bytes 147460
  197.2 7.2 %collective-permute-start.38 = (bf16[96,256]{1,0:T(8,128)(2,1)S(1)}, bf16[96,256]{1,0:T(8,128)(2,1)S(1)}, u32[]{:S(2)}, u32[]{:S(2)}) collective-permute-start(bf16[96,256]{1,0:T(8,128)(2,1)S(1)} %add_add_fusion.a_ref), channel_id=1, source_target_pairs={{0,8},{2,10},{4,12},{6,14},{8,0},{10,2},{12,4},{14,6},{16,24},{18,... | collective-permute-start | bytes 147464 | tf_op jit(solution)/shard_map/ppermute | solution.py:864
  197.8 6.6 %collective-permute-start.39 = (bf16[96,256]{1,0:T(8,128)(2,1)S(1)}, bf16[96,256]{1,0:T(8,128)(2,1)S(1)}, u32[]{:S(2)}, u32[]{:S(2)}) collective-permute-start(bf16[96,256]{1,0:T(8,128)(2,1)S(1)} %add_add_fusion.a_ref), channel_id=1, source_target_pairs={{0,16},{2,18},{4,20},{6,22},{8,24},{10,26},{12,28},{14,30},{16,0},... | collective-permute-start | bytes 147464 | tf_op jit(solution)/shard_map/ppermute | solution.py:864
  199.5 5.9 %collective-permute-start.40 = (bf16[96,256]{1,0:T(8,128)(2,1)S(1)}, bf16[96,256]{1,0:T(8,128)(2,1)S(1)}, u32[]{:S(2)}, u32[]{:S(2)}) collective-permute-start(bf16[96,256]{1,0:T(8,128)(2,1)S(1)} %add_add_fusion.a_ref), channel_id=1, source_target_pairs={{0,24},{2,26},{4,28},{6,30},{8,16},{10,18},{12,20},{14,22},{16,8},... | collective-permute-start | bytes 147464 | tf_op jit(solution)/shard_map/ppermute | solution.py:864
  202.4 6.3 %copy-start.1 = (s32[4,392]{1,0:T(4,128)S(1)}, s32[4,392]{1,0:T(4,128)}, u32[]{:S(2)}) copy-start(s32[4,392]{1,0:T(4,128)} %param.36) | copy-start | bytes 18820
  203.2 4.7 %collective-permute-start.43 = (bf16[64,768]{1,0:T(8,128)(2,1)S(1)}, bf16[64,768]{1,0:T(8,128)(2,1)S(1)}, u32[]{:S(2)}, u32[]{:S(2)}) collective-permute-start(bf16[64,768]{1,0:T(8,128)(2,1)S(1)} %fusion.5), channel_id=1, source_target_pairs={{0,2},{2,0},{1,3},{3,1},{4,6},{6,4},{5,7},{7,5},{8,10},{10,8},{9,1... | collective-permute-start | bytes 294920 | tf_op jit(solution)/shard_map/ppermute | solution.py:766
  (17 other events, 24.8 us)
where the time goes:
time: 210 us; the launch traced here: 209 us
  Pallas kernels  121 us (58%)
  starting transfers between devices  38.3 us (18%)
  waiting for transfers between devices  23.3 us (11%)
  other arithmetic  13.6 us (6%)
  local copies, waits for them, and re-layouts  11.6 us (6%)
    ppermute x36, starting transfers between devices, swap(): return lax.ppermute(value, axis, pairs)  28.7 us
    pallas_call x2, Pallas kernels, attend_back(): pl.pallas_call(functools.partial(attend_back_kernel, scale), grid_spec=pl...  22.9 us
    ppermute x36, waiting for transfers between devices, swap(): return lax.ppermute(value, axis, pairs)  21.4 us
    pallas_call x2, Pallas kernels, fold(): pl.pallas_call(functools.partial(fold_end_kernel if extra else fold_start...  18.4 us
    pallas_call x2, Pallas kernels, lookup(): pl.pallas_call(functools.partial(lookup_kernel, heads), grid=(count,), in...  17.1 us
    pallas_call x1, Pallas kernels, middle_back(): pl.pallas_call(middle_back_kernel, grid=(wins,), in_specs=[window_spec(a,...  16.2 us
    pallas_call x1, Pallas kernels, attend(): pl.pallas_call(attend_kernel, grid_spec=pltpu.PrefetchScalarGridSpec(num_...  15.2 us
    ppermute x6, starting transfers between devices, joint_swap(): lax.ppermute(value, ('shard', 'ctx'), [(i, i ^ mask) for i in range(size)])  8.01 us
  transfers between devices with their start and end apart: 44, of which 13 were waited for; matrix products, arithmetic and copies ran while one was open for 9% of the time, Pallas kernels for 47%

commit v1 on v0

--- a/solution.py
+++ b/solution.py
@@ -1048,9 +1048,9 @@
     rest = gather_join(rest, first, rest_got)
     rest, rest_got = gather_send(rest, middle)
     qkv_got = swap(qkv, "shard", last)
-    xm, cm, other = shift_in(pair_rows, pair_got, clips, counts, core_row)
-    bias_own = lookup(after(index, xm), own, got, heads, early_blocks, block - early_blocks, (part_own,))
-    rest_got, qkv_got, other, bias_own = joint((rest_got, qkv_got, other, bias_own), ())
+    bias_own = lookup(index, own, got, heads, early_blocks, block - early_blocks, (part_own,))
+    rest_got, qkv_got, bias_own = joint((rest_got, qkv_got, bias_own), ())
+    xm, cm, other = shift_in(pair_rows, after(pair_got, bias_own), clips, counts, core_row)
     qkv = gather_join(qkv, last, qkv_got)
     qkv = qkv.reshape(-1, qkv.shape[-1])
     qkv_other = swap(qkv, "tensor")

time: 210 us -> 207 us (0.986)
  waiting for transfers between devices: 23.3 us -> 16.2 us
  local copies, waits for them, and re-layouts: 11.6 us -> 15.7 us
    ppermute x36, waiting for transfers between devices: 21.4 us -> 16.2 us  [swap(): return lax.ppermute(value, axis, pairs)]
    unnamed x76 -> x102, local copies, waits for them, and re-layouts: 4.91 us -> 9.61 us
  transfers between devices with their start and end apart: 44 -> 44, of which waited for: 13 -> 9; matrix products, arithmetic and copies ran while one was open for 9% -> 8% of each run, Pallas kernels for 47% -> 49%
where the time goes in v1:
time: 207 us; the launch traced here: 206 us
  Pallas kernels  121 us (58%)
  starting transfers between devices  39.3 us (19%)
  waiting for transfers between devices  16.2 us (8%)
  local copies, waits for them, and re-layouts  15.7 us (8%)
  other arithmetic  12.5 us (6%)
    ppermute x36, starting transfers between devices, swap(): return lax.ppermute(value, axis, pairs)  29.5 us
    pallas_call x2, Pallas kernels, attend_back(): pl.pallas_call(functools.partial(attend_back_kernel, scale), grid_spec=pl...  22.7 us
    pallas_call x2, Pallas kernels, fold(): pl.pallas_call(functools.partial(fold_end_kernel if extra else fold_start...  18.3 us
    pallas_call x2, Pallas kernels, lookup(): pl.pallas_call(functools.partial(lookup_kernel, heads), grid=(count,), in...  17 us
    pallas_call x1, Pallas kernels, middle_back(): pl.pallas_call(middle_back_kernel, grid=(wins,), in_specs=[window_spec(a,...  16.2 us
    ppermute x36, waiting for transfers between devices, swap(): return lax.ppermute(value, axis, pairs)  16.2 us
    pallas_call x1, Pallas kernels, attend(): pl.pallas_call(attend_kernel, grid_spec=pltpu.PrefetchScalarGridSpec(num_...  15.3 us
    unnamed x102, local copies, waits for them, and re-layouts  9.61 us
  transfers between devices with their start and end apart: 44, of which 9 were waited for; matrix products, arithmetic and copies ran while one was open for 8% of the time, Pallas kernels for 49%

profile of v1, /device:TPU:0, one launch (start us, length us, event | category | flops | bytes accessed | tf_op | source)
XLA Modules:
  0.0 206.3 jit_solution(11433273908664152561)
XLA Ops:
  0.7 1.1 copy.37
  1.8 4.1 %collective-permute-start = (bf16[1,1,1,64,768]{4,3,2,1,0:T(8,128)(2,1)S(1)}, bf16[1,1,1,64,768]{4,3,2,1,0:T(8,128)(2,1)S(1)}, u32[]{:S(2)}, u32[]{:S(2)}) collective-permute-start(bf16[1,1,1,64,768]{4,3,2,1,0:T(8,128)(2,1)S(1)} %reshape_reshape.3), channel_id=1, source_target_pairs={{0,16},{4,20},{8,24},{12,28},{16,0},{20,4},{24,8},{28,12},{1,17},{... | collective-permute-start | bytes 294920 | tf_op jit(solution)/shard_map/ppermute | solution.py:766
  5.9 1.0 slice.32
  7.1 1.0 pad_maximum_fusion.3
  8.0 1.5 collective-permute-start.2
  9.6 1.7 pack.1.own_ref
  11.3 1.4 copy.38
  12.7 0.8 pad_dynamic-slice_fusion.idx_ref
  14.0 1.6 collective-permute-start.1
  15.6 1.3 collective-permute-done.4.got_ref
  17.5 6.9 %table_lookup.2.rest_0_ = bf16[16,208,512]{2,1,0:T(8,128)(2,1)} custom-call(s32[208,400]{1,0:T(8,128)} %pad_dynamic-slice_fusion.idx_ref, f32[96,256]{1,0:T(8,128)} %pack.1.own_ref, f32[96,256]{1,0:T(8,128)} %copy-done.10), custom_call_target="tpu_custom_call" | custom-call | flops 1 | bytes 1 | tf_op jit(solution)/shard_map/table_lookup/pallas_call | solution.py:177
  24.4 4.7 %collective-permute-done.3 = bf16[1,1,1,64,2304]{4,3,2,1,0:T(8,128)(2,1)S(1)} collective-permute-done((bf16[1,1,1,64,2304]{4,3,2,1,0:T(8,128)(2,1)S(1)}, bf16[1,1,1,64,2304]{4,3,2,1,0:T(8,128)(2,1)S(1)}, u32[]{:S(2)}, u32[]{:S(2)}) %collective-permute-start.3) | collective-permute-done | bytes 294944 | tf_op jit(solution)/shard_map/ppermute | solution.py:766
  30.0 1.6 collective-permute-start.6
  31.6 10.1 %table_lookup.3.own_ref = bf16[16,208,512]{2,1,0:T(8,128)(2,1)} custom-call(s32[208,400]{1,0:T(8,128)} %pad_dynamic-slice_fusion.idx_ref, f32[96,256]{1,0:T(8,128)} %pack.1.own_ref, f32[96,256]{1,0:T(8,128)} %copy-done.10, bf16[16,208,512]{2,1,0:T(8,128)(2,1)} %table_lookup.2.rest_0_), custom_call_target="tpu_custom_call", output_to_operand_aliasing={{}: (3, {})} | custom-call | flops 1 | bytes 1 | tf_op jit(solution)/shard_map/table_lookup/pallas_call | solution.py:177
  41.7 1.8 collective-permute-done.5
  43.6 0.8 copy-done.21
  44.4 1.1 pad_maximum_fusion
  45.5 1.5 collective-permute-start.8
  47.0 1.1 copy-done.16
  48.2 2.8 %select_in.1 = (bf16[2,400,256]{2,1,0:T(8,128)(2,1)S(1)}, bf16[2,400,256]{2,1,0:T(8,128)(2,1)S(1)}, bf16[4,400,256]{2,1,0:T(8,128)(2,1)}) custom-call(s32[1]{0:T(128)} %bitcast.core_ref, s32[2,1632,1]{2,1,0:T(8,128)S(1)} %copy-done.14, bf16[4,392,256]{2,1,0:T(8,128)(2,1)S(1)} %bitcast.54, bf16[4,392,256]{2,1,0:T(8,128)(2,1)S(1)} %bitcast.56, ...), custom_call_target="tpu_custom_call" | custom-call | flops 1 | bytes 1 | tf_op jit(solution)/shard_map/select_in/pallas_call | solution.py:710
  52.8 1.7 collective-permute-done.9.wo_ref
  54.5 0.9 copy-done.26
  55.7 4.9 %front.1 = (bf16[2,512,400]{2,1,0:T(8,128)(2,1)}, bf16[2,512,400]{2,1,0:T(8,128)(2,1)}, bf16[2,512,400]{2,1,0:T(8,128)(2,1)}, bf16[2,512,400]{2,1,0:T(8,128)(2,1)}) custom-call(bf16[2,400,256]{2,1,0:T(8,128)(2,1)} %copy-done.8, bf16[4,400,256]{2,1,0:T(8,128)(2,1)} %copy-done.2, f32[96,256]{1,0:T(8,128)} %pack.1.own_ref, f32[96,256]{1,0:T(8,128)} %copy-done.10, ...), custom_call_target="tpu_custom_call" | custom-call | flops 1 | bytes 1 | tf_op jit(solution)/shard_map/front/pallas_call | solution.py:451
  60.6 15.3 %attend.1 = (bf16[2,512,400]{2,1,0:T(8,128)(2,1)}, f32[2,512,400]{2,1,0:T(8,128)}, f32[2,4,4,400]{3,2,1,0:T(4,128)}) custom-call(s32[1]{0:T(128)} %bitcast.core_ref, bf16[2,512,400]{2,1,0:T(8,128)(2,1)} %get-tuple-element.143.q_ref, bf16[2,512,400]{2,1,0:T(8,128)(2,1)} %get-tuple-element.144.k_ref, bf16[2,512,400]{2,1,0:T(8,128)(2,1)} %get-tuple-element.145.v_ref, ...), custom_call_target="tpu_custom_call" | custom-call | flops 1 | bytes 1 | tf_op jit(solution)/shard_map/attend/pallas_call | solution.py:338
  75.9 1.3 broadcast_select_fusion.1
  77.5 1.2 broadcast_select_fusion.5
  79.2 1.1 collective-permute-done.11.wo_ref
  80.4 4.6 %middle_forward.1 = (f32[2,400,512]{2,1,0:T(8,128)S(1)}, bf16[2,400,512]{2,1,0:T(8,128)(2,1)S(1)}, bf16[2,400,2048]{2,1,0:T(8,128)(2,1)S(1)}, bf16[2,400,2048]{2,1,0:T(8,128)(2,1)S(1)}) custom-call(bf16[2,400,256]{2,1,0:T(8,128)(2,1)S(1)} %copy-done.9, bf16[4,400,256]{2,1,0:T(8,128)(2,1)S(1)} %copy-done.3, bf16[2,512,400]{2,1,0:T(8,128)(2,1)S(1)} %copy-done.7, ...), custom_call_target="tpu_custom_call" | custom-call | flops 1 | bytes 1 | tf_op jit(solution)/shard_map/middle_forward/pallas_call | solution.py:493
  85.0 16.2 %middle_back.1 = (bf16[2,208,256]{2,1,0:T(8,128)(2,1)}, bf16[2,208,256]{2,1,0:T(8,128)(2,1)}, bf16[2,208,256]{2,1,0:T(8,128)(2,1)}, bf16[2,208,256]{2,1,0:T(8,12...) custom-call(bf16[2,400,256]{2,1,0:T(8,128)(2,1)S(1)} %copy-done.18, ...), custom_call_target="tpu_custom_call" | custom-call | flops 1 | bytes 1 | tf_op jit(solution)/shard_map/middle_back/pallas_call | solution.py:586
  102.4 1.2 collective-permute-start.17
  103.7 11.2 %attend_back.2 = (bf16[2,256,400]{2,1,0:T(8,128)(2,1)}, bf16[2,256,400]{2,1,0:T(8,128)(2,1)}, bf16[2,256,400]{2,1,0:T(8,128)(2,1)}, bf16[8,208,512]{2,1,0:T(8,128)(2,1)}, bf16[8,208,512]{2,1,0:T(8,128)(2,1)}) custom-call(s32[1]{0:T(128)} %bitcast.core_ref, bf16[2,512,400]{2,1,0:T(8,128)(2,1)} %get-tuple-element.143.q_ref, ...), custom_call_target="tpu_custom_call" | custom-call | flops 1 | bytes 1 | tf_op jit(solution)/shard_map/attend_back/pallas_call | solution.py:415
  115.0 4.0 %side_grads.1 = bf16[512,768]{1,0:T(8,128)(2,1)} custom-call(bf16[2,512,400]{2,1,0:T(8,128)(2,1)} %get-tuple-element.167.first_ref, bf16[2,256,400]{2,1,0:T(8,128)(2,1)} %get-tuple-element.168.dq_ref.qo_ref, bf16[2,256,400]{2,1,0:T(8,128)(2,1)} %get-tuple-element.169.dk_ref.ko_ref, bf16[2,256,400]{2,1,0:T(8,128)(2,1)} %get-tuple-element.170.dv_ref.vo_ref), custom_call_target="tpu_custom_call" | custom-call | flops 1 | bytes 1 | tf_op jit(solution)/shard_map/side_grads/pallas_call | solution.py:608
  121.6 0.7 collective-permute-start.18
  122.4 11.4 %attend_back.3 = (bf16[2,256,400]{2,1,0:T(8,128)(2,1)}, bf16[2,256,400]{2,1,0:T(8,128)(2,1)}, bf16[2,256,400]{2,1,0:T(8,128)(2,1)}, bf16[8,208,512]{2,1,0:T(8,128)(2,1)}, bf16[8,208,512]{2,1,0:T(8,128)(2,1)}) custom-call(s32[1]{0:T(128)} %bitcast.core_ref, bf16[2,512,400]{2,1,0:T(8,128)(2,1)} %get-tuple-element.143.q_ref, ...), custom_call_target="tpu_custom_call" | custom-call | flops 1 | bytes 1 | tf_op jit(solution)/shard_map/attend_back/pallas_call | solution.py:415
  133.8 2.2 %collective-permute-done.18 = bf16[2,2,1,64,1024]{4,3,2,1,0:T(8,128)(2,1)S(1)} collective-permute-done((bf16[2,2,1,64,1024]{4,3,2,1,0:T(8,128)(2,1)S(1)}, bf16[2,2,1,64,1024]{4,3,2,1,0:T(8,128)(2,1)S(1)}, u32[]{:S(2)}, u32[]{:S(2)}) %collective-permute-start.18) | collective-permute-done | bytes 524320 | tf_op jit(solution)/shard_map/ppermute | solution.py:766
  135.9 1.2 collective-permute-done.19
  137.3 1.3 add_convert_fusion.2
  138.7 0.7 collective-permute-start.23
  139.6 0.8 copy-done.29
  140.4 0.7 constant_dynamic-slice_fusion.6
  141.4 7.9 %back.1 = (bf16[2,208,256]{2,1,0:T(8,128)(2,1)}, bf16[2,208,256]{2,1,0:T(8,128)(2,1)}, bf16[2,208,256]{2,1,0:T(8,128)(2,1)}, bf16[2,208,256]{2,1,0:T(8,128)(2,1)...) custom-call(s32[1]{0:T(128)} %bitcast.18.place_ref, bf16[2,400,256]{2,1,0:T(8,128)(2,1)} %copy-done.8, ...), custom_call_target="tpu_custom_call" | custom-call | flops 1 | bytes 1 | tf_op jit(solution)/shard_map/back/pallas_call | solution.py:661
  149.3 1.4 collective-permute-start.25
  150.8 2.2 %select_out.2 = f32[4,392,256]{2,1,0:T(8,128)} custom-call(s32[1]{0:T(128)} %bitcast.core_ref, s32[2,1600,1]{2,1,0:T(8,128)S(1)} %copy-done.4, bf16[416,256]{1,0:T(8,128)(2,1)S(1)} %bitcast.57, bf16[416,256]{1,0:T(8,128)(2,1)S(1)} %collective-permute-done.15.beside_ref, bf16[416,256]{1,0:T(8,128)(2,1)S(1)} %collective-permute-done.16.across_ref, ...), custom_call_target="tpu_custom_call" | custom-call | flops 1 | bytes 1 | tf_op jit(solution)/shard_map/select_out/pallas_call | solution.py:741
  153.0 1.3 collective-permute-start.29
  155.0 1.8 collective-permute-start.26
  156.8 1.0 add_convert_fusion.5
  157.8 1.1 collective-permute-start.27
  158.9 8.5 %table_fold.2.init_ref = f32[160,256]{1,0:T(8,128)} custom-call(s32[1]{0:T(128)} %bitcast.core_ref, s32[208,400]{1,0:T(8,128)} %pad_dynamic-slice_fusion.idx_ref, bf16[8,208,512]{2,1,0:T(8,128)(2,1)} %get-tuple-element.196.pair_m, bf16[8,208,512]{2,1,0:T(8,128)(2,1)} %get-tuple-element.197.pair_o, bf16[8,208,512]{2,1,0:T(8,128)(2,1)} %collective-permute-done.24.sent_m, ...), custom_call_target="tpu_custom_call" | custom-call | flops 1 | bytes 1 | tf_op jit(solution)/shard_map/table_fold/pallas_call | solution.py:252
  168.2 1.1 fusion
  169.3 1.8 collective-permute-start.31
  171.1 1.2 collective-permute-start.32
  172.4 9.8 %table_fold.3 = (f32[96,256]{1,0:T(8,128)}, f32[96,256]{1,0:T(8,128)}) custom-call(s32[1]{0:T(128)} %bitcast.core_ref, s32[208,400]{1,0:T(8,128)} %pad_dynamic-slice_fusion.idx_ref, bf16[8,208,512]{2,1,0:T(8,128)(2,1)} %get-tuple-element.196.pair_m, bf16[8,208,512]{2,1,0:T(8,128)(2,1)} %get-tuple-element.197.pair_o, ...), custom_call_target="tpu_custom_call" | custom-call | flops 1 | bytes 1 | tf_op jit(solution)/shard_map/table_fold/pallas_call | solution.py:252
  182.2 0.9 collective-permute-start.42
  183.2 1.5 collective-permute-done.34
  184.7 0.9 add.160
  185.6 1.2 collective-permute-start.35
  187.5 1.6 collective-permute-start.37
  189.2 2.4 %collective-permute-start.41 = (bf16[1,1,1,64,768]{4,3,2,1,0:T(8,128)(2,1)S(1)}, bf16[1,1,1,64,768]{4,3,2,1,0:T(8,128)(2,1)S(1)}, u32[]{:S(2)}, u32[]{:S(2)}) collective-permute-start(bf16[1,1,1,64,768]{4,3,2,1,0:T(8,128)(2,1)S(1)} %constant_dynamic-slice_fusion), channel_id=1, source_target_pairs={{0,16},{4,20},{8,24},{12,28},{16,0},{20,4},{24,8},{28,12},{1,17},{... | collective-permute-start | bytes 294920 | tf_op jit(solution)/shard_map/ppermute | solution.py:766
  191.6 2.2 %select_out.3 = f32[4,392,256]{2,1,0:T(8,128)} custom-call(s32[1]{0:T(128)} %bitcast.core_ref, s32[2,1600,1]{2,1,0:T(8,128)S(1)} %copy-done.4, bf16[416,256]{1,0:T(8,128)(2,1)S(1)} %bitcast.58, bf16[416,256]{1,0:T(8,128)(2,1)S(1)} %collective-permute-done.28.beside_ref, bf16[416,256]{1,0:T(8,128)(2,1)S(1)} %collective-permute-done.29.across_ref, ...), custom_call_target="tpu_custom_call" | custom-call | flops 1 | bytes 1 | tf_op jit(solution)/shard_map/select_out/pallas_call | solution.py:741
  194.2 1.9 collective-permute-start.39
  196.1 2.2 %collective-permute-start.40 = (bf16[96,256]{1,0:T(8,128)(2,1)S(1)}, bf16[96,256]{1,0:T(8,128)(2,1)S(1)}, u32[]{:S(2)}, u32[]{:S(2)}) collective-permute-start(bf16[96,256]{1,0:T(8,128)(2,1)S(1)} %add_add_fusion.a_ref), channel_id=1, source_target_pairs={{0,24},{2,26},{4,28},{6,30},{8,16},{10,18},{12,20},{14,22},{16,8},... | collective-permute-start | bytes 147464 | tf_op jit(solution)/shard_map/ppermute | solution.py:864
  198.3 1.7 convert_add_fusion.1
  200.0 0.7 slice_bitcast_fusion
  203.2 1.5 unpack.1
  (197 shorter events, 16.3 us)
Async XLA Ops:
  0.6 51.5 %copy-start = (s32[4,392]{1,0:T(4,128)S(1)}, s32[4,392]{1,0:T(4,128)}, u32[]{:S(2)}) copy-start(s32[4,392]{1,0:T(4,128)} %param.36) | copy-start | bytes 18820
  0.7 6.4 %copy-start.13 = (bf16[1,4,392,256]{3,2,1,0:T(8,128)(2,1)S(1)}, bf16[1,4,392,256]{3,2,1,0:T(8,128)(2,1)}, u32[]{:S(2)}) copy-start(bf16[1,4,392,256]{3,2,1,0:T(8,128)(2,1)} %param.21) | copy-start | bytes 2408452
  1.8 11.7 %collective-permute-start = (bf16[1,1,1,64,768]{4,3,2,1,0:T(8,128)(2,1)S(1)}, bf16[1,1,1,64,768]{4,3,2,1,0:T(8,128)(2,1)S(1)}, u32[]{:S(2)}, u32[]{:S(2)}) collective-permute-start(bf16[1,1,1,64,768]{4,3,2,1,0:T(8,128)(2,1)S(1)} %reshape_reshape.3), channel_id=1, source_target_pairs={{0,16},{4,20},{8,24},{12,28},{16,0},{20,4},{24,8},{28,12},{1,17},{... | collective-permute-start | bytes 294920 | tf_op jit(solution)/shard_map/ppermute | solution.py:766
  8.0 21.1 %collective-permute-start.2 = (bf16[1600,256]{1,0:T(8,128)(2,1)}, bf16[1600,256]{1,0:T(8,128)(2,1)S(1)}, u32[]{:S(2)}, u32[]{:S(2)}) collective-permute-start(bf16[1600,256]{1,0:T(8,128)(2,1)} %bitcast.5), channel_id=1, source_target_pairs={{0,2},{2,0},{1,3},{3,1},{4,6},{6,4},{5,7},{7,5},{8,10},{10,8},{9,1... | collective-permute-start | bytes 2457608 | tf_op jit(solution)/shard_map/ppermute | solution.py:766
  13.6 15.5 %collective-permute-start.3 = (bf16[1,1,1,64,2304]{4,3,2,1,0:T(8,128)(2,1)S(1)}, bf16[1,1,1,64,2304]{4,3,2,1,0:T(8,128)(2,1)S(1)}, u32[]{:S(2)}, u32[]{:S(2)}) collective-permute-start(bf16[1,1,1,64,2304]{4,3,2,1,0:T(8,128)(2,1)S(1)} %maximum_bitcast_fusion), channel_id=1, source_target_pairs={{0,16},{4,20},{8,24},{12,28},{16,0},{20,4},{24,8},{28,12},{1,17},{... | collective-permute-start | bytes 884744 | tf_op jit(solution)/shard_map/ppermute | solution.py:766
  14.0 10.4 %collective-permute-start.1 = (bf16[2,1,1,64,768]{4,3,2,1,0:T(8,128)(2,1)S(1)}, bf16[2,1,1,64,768]{4,3,2,1,0:T(8,128)(2,1)S(1)}, u32[]{:S(2)}, u32[]{:S(2)}) collective-permute-start(bf16[2,1,1,64,768]{4,3,2,1,0:T(8,128)(2,1)S(1)} %pad_maximum_fusion.7), channel_id=1, source_target_pairs={{0,8},{4,12},{8,0},{12,4},{16,24},{20,28},{24,16},{28,20},{1,9},{5... | collective-permute-start | bytes 589832 | tf_op jit(solution)/shard_map/ppermute | solution.py:766
  15.6 1.3 collective-permute-start.4
  29.2 14.3 %collective-permute-start.5 = (bf16[2,1,1,64,2304]{4,3,2,1,0:T(8,128)(2,1)S(1)}, bf16[2,1,1,64,2304]{4,3,2,1,0:T(8,128)(2,1)S(1)}, u32[]{:S(2)}, u32[]{:S(2)}) collective-permute-start(bf16[2,1,1,64,2304]{4,3,2,1,0:T(8,128)(2,1)S(1)} %pad_maximum_fusion.5), channel_id=1, source_target_pairs={{0,8},{4,12},{8,0},{12,4},{16,24},{20,28},{24,16},{28,20},{1,9},{5... | collective-permute-start | bytes 1769480 | tf_op jit(solution)/shard_map/ppermute | solution.py:766
  30.0 11.7 %copy-start.31 = (bf16[2,1,1,64,768]{4,3,2,1,0:T(8,128)(2,1)}, bf16[2,1,1,64,768]{4,3,2,1,0:T(8,128)(2,1)S(1)}, u32[]{:S(2)}) copy-start(bf16[2,1,1,64,768]{4,3,2,1,0:T(8,128)(2,1)S(1)} %get-tuple-element.265) | copy-start | bytes 589828
  30.0 11.6 %collective-permute-start.6 = (bf16[2,2,1,64,768]{4,3,2,1,0:T(8,128)(2,1)S(1)}, bf16[2,2,1,64,768]{4,3,2,1,0:T(8,128)(2,1)S(1)}, u32[]{:S(2)}, u32[]{:S(2)}) collective-permute-start(bf16[2,2,1,64,768]{4,3,2,1,0:T(8,128)(2,1)S(1)} %pad_maximum_fusion.6), channel_id=1, source_target_pairs={{0,4},{4,0},{8,12},{12,8},{16,20},{20,16},{24,28},{28,24},{1,5},{5... | collective-permute-start | bytes 1179656 | tf_op jit(solution)/shard_map/ppermute | solution.py:766
  43.5 17.1 %collective-permute-start.10 = (bf16[16,208,512]{2,1,0:T(8,128)(2,1)}, bf16[16,208,512]{2,1,0:T(8,128)(2,1)}, u32[]{:S(2)}, u32[]{:S(2)}) collective-permute-start(bf16[16,208,512]{2,1,0:T(8,128)(2,1)} %table_lookup.3.own_ref), channel_id=1, source_target_pairs={{0,1},{1,0},{2,3},{3,2},{4,5},{5,4},{6,7},{7,6},{8,9},{9,8},{10,11... | collective-permute-start | bytes 10223624 | tf_op jit(solution)/shard_map/ppermute | solution.py:766
  43.5 3.5 %copy-start.14 = (s32[2,1632,1]{2,1,0:T(8,128)S(1)}, s32[2,1632,1]{2,1,0:T(8,128)}, u32[]{:S(2)}) copy-start(s32[2,1632,1]{2,1,0:T(8,128)} %constant.103.clone.picks_ref) | copy-start | bytes 39172
  43.6 3.4 %copy-start.12 = (bf16[1,4,392,256]{3,2,1,0:T(8,128)(2,1)S(1)}, bf16[1,4,392,256]{3,2,1,0:T(8,128)(2,1)}, u32[]{:S(2)}) copy-start(bf16[1,4,392,256]{3,2,1,0:T(8,128)(2,1)} %param.20) | copy-start | bytes 2408452
  45.5 30.3 %collective-permute-start.8 = (bf16[2,2,1,64,2304]{4,3,2,1,0:T(8,128)(2,1)}, bf16[2,2,1,64,2304]{4,3,2,1,0:T(8,128)(2,1)}, u32[]{:S(2)}, u32[]{:S(2)}) collective-permute-start(bf16[2,2,1,64,2304]{4,3,2,1,0:T(8,128)(2,1)} %pad_maximum_fusion), channel_id=1, source_target_pairs={{0,4},{4,0},{8,12},{12,8},{16,20},{20,16},{24,28},{28,24},{1,5},{5... | collective-permute-start | bytes 3538952 | tf_op jit(solution)/shard_map/ppermute | solution.py:766
  48.2 3.1 %copy-start.41 = (bf16[2,2,1,64,768]{4,3,2,1,0:T(8,128)(2,1)S(1)}, bf16[2,2,1,64,768]{4,3,2,1,0:T(8,128)(2,1)}, u32[]{:S(2)}) copy-start(bf16[2,2,1,64,768]{4,3,2,1,0:T(8,128)(2,1)} %copy-done.40) | copy-start | bytes 1179652
  51.0 3.5 %collective-permute-start.7 = (bf16[4,400,256]{2,1,0:T(8,128)(2,1)}, bf16[4,400,256]{2,1,0:T(8,128)(2,1)S(1)}, u32[]{:S(2)}, u32[]{:S(2)}) collective-permute-start(bf16[4,400,256]{2,1,0:T(8,128)(2,1)} %get-tuple-element.139), channel_id=1, source_target_pairs={{0,1},{1,0},{2,3},{3,2},{4,5},{5,4},{6,7},{7,6},{8,9},{9,8},{10,11... | collective-permute-start | bytes 2457608 | tf_op jit(solution)/shard_map/ppermute | solution.py:766
  51.9 2.6 %collective-permute-start.9 = (bf16[512,768]{1,0:T(8,128)(2,1)S(1)}, bf16[512,768]{1,0:T(8,128)(2,1)S(1)}, u32[]{:S(2)}, u32[]{:S(2)}) collective-permute-start(bf16[512,768]{1,0:T(8,128)(2,1)S(1)} %bitcast.59), channel_id=1, source_target_pairs={{0,1},{1,0},{2,3},{3,2},{4,5},{5,4},{6,7},{7,6},{8,9},{9,8},{10,11... | collective-permute-start | bytes 2359304 | tf_op jit(solution)/shard_map/ppermute | solution.py:766
  60.5 15.3 %copy-start.22 = (bf16[2,1,1,64,2304]{4,3,2,1,0:T(8,128)(2,1)S(1)}, bf16[2,1,1,64,2304]{4,3,2,1,0:T(8,128)(2,1)}, u32[]{:S(2)}) copy-start(bf16[2,1,1,64,2304]{4,3,2,1,0:T(8,128)(2,1)} %copy-done.21) | copy-start | bytes 1769476
  60.6 15.3 %copy-start.24 = (bf16[2,1,1,64,2304]{4,3,2,1,0:T(8,128)(2,1)S(1)}, bf16[2,1,1,64,2304]{4,3,2,1,0:T(8,128)(2,1)}, u32[]{:S(2)}) copy-start(bf16[2,1,1,64,2304]{4,3,2,1,0:T(8,128)(2,1)} %copy-done.23) | copy-start | bytes 1769476
  77.3 3.1 %collective-permute-start.11 = (bf16[512,1280]{1,0:T(8,128)(2,1)S(1)}, bf16[512,1280]{1,0:T(8,128)(2,1)S(1)}, u32[]{:S(2)}, u32[]{:S(2)}) collective-permute-start(bf16[512,1280]{1,0:T(8,128)(2,1)S(1)} %bitcast.48), channel_id=1, source_target_pairs={{0,1},{1,0},{2,3},{3,2},{4,5},{5,4},{6,7},{7,6},{8,9},{9,8},{10,11... | collective-permute-start | bytes 3932168 | tf_op jit(solution)/shard_map/ppermute | solution.py:766
  78.9 6.1 %copy-start.18 = (bf16[2,400,256]{2,1,0:T(8,128)(2,1)S(1)}, bf16[2,400,256]{2,1,0:T(8,128)(2,1)}, u32[]{:S(2)}) copy-start(bf16[2,400,256]{2,1,0:T(8,128)(2,1)} %copy-done.17) | copy-start | bytes 1228804
  78.9 6.1 %collective-permute-start.12 = (bf16[512,1024]{1,0:T(8,128)(2,1)S(1)}, bf16[512,1024]{1,0:T(8,128)(2,1)S(1)}, u32[]{:S(2)}, u32[]{:S(2)}) collective-permute-start(bf16[512,1024]{1,0:T(8,128)(2,1)S(1)} %bitcast.51), channel_id=1, source_target_pairs={{0,1},{1,0},{2,3},{3,2},{4,5},{5,4},{6,7},{7,6},{8,9},{9,8},{10,11... | collective-permute-start | bytes 3145736 | tf_op jit(solution)/shard_map/ppermute | solution.py:766
  101.2 13.7 %collective-permute-start.14 = (bf16[512,1280]{1,0:T(8,128)(2,1)}, bf16[512,1280]{1,0:T(8,128)(2,1)S(1)}, u32[]{:S(2)}, u32[]{:S(2)}) collective-permute-start(bf16[512,1280]{1,0:T(8,128)(2,1)} %get-tuple-element.155), channel_id=1, source_target_pairs={{0,1},{1,0},{2,3},{3,2},{4,5},{5,4},{6,7},{7,6},{8,9},{9,8},{10,11... | collective-permute-start | bytes 3932168 | tf_op jit(solution)/shard_map/ppermute | solution.py:766
  101.5 13.4 %collective-permute-start.13 = (bf16[512,1024]{1,0:T(8,128)(2,1)}, bf16[512,1024]{1,0:T(8,128)(2,1)S(1)}, u32[]{:S(2)}, u32[]{:S(2)}) collective-permute-start(bf16[512,1024]{1,0:T(8,128)(2,1)} %get-tuple-element.154), channel_id=1, source_target_pairs={{0,1},{1,0},{2,3},{3,2},{4,5},{5,4},{6,7},{7,6},{8,9},{9,8},{10,11... | collective-permute-start | bytes 3145736 | tf_op jit(solution)/shard_map/ppermute | solution.py:766
  101.8 13.1 %collective-permute-start.15 = (bf16[416,256]{1,0:T(8,128)(2,1)}, bf16[416,256]{1,0:T(8,128)(2,1)S(1)}, u32[]{:S(2)}, u32[]{:S(2)}) collective-permute-start(bf16[416,256]{1,0:T(8,128)(2,1)} %bitcast.77), channel_id=1, source_target_pairs={{0,1},{1,0},{2,3},{3,2},{4,5},{5,4},{6,7},{7,6},{8,9},{9,8},{10,11... | collective-permute-start | bytes 638984 | tf_op jit(solution)/shard_map/ppermute | solution.py:766
  102.0 12.9 %collective-permute-start.16 = (bf16[416,256]{1,0:T(8,128)(2,1)}, bf16[416,256]{1,0:T(8,128)(2,1)S(1)}, u32[]{:S(2)}, u32[]{:S(2)}) collective-permute-start(bf16[416,256]{1,0:T(8,128)(2,1)} %bitcast.76), channel_id=1, source_target_pairs={{0,2},{2,0},{1,3},{3,1},{4,6},{6,4},{5,7},{7,5},{8,10},{10,8},{9,1... | collective-permute-start | bytes 638984 | tf_op jit(solution)/shard_map/ppermute | solution.py:766
  102.4 12.5 %collective-permute-start.17 = (bf16[416,256]{1,0:T(8,128)(2,1)}, bf16[416,256]{1,0:T(8,128)(2,1)S(1)}, u32[]{:S(2)}, u32[]{:S(2)}) collective-permute-start(bf16[416,256]{1,0:T(8,128)(2,1)} %bitcast.75), channel_id=1, source_target_pairs={{0,3},{1,2},{2,1},{3,0},{4,7},{5,6},{6,5},{7,4},{8,11},{9,10},{10,... | collective-permute-start | bytes 638984 | tf_op jit(solution)/shard_map/ppermute | solution.py:978
  114.9 4.0 %copy-start.35 = (bf16[512,1024]{1,0:T(8,128)(2,1)}, bf16[512,1024]{1,0:T(8,128)(2,1)S(1)}, u32[]{:S(2)}) copy-start(bf16[512,1024]{1,0:T(8,128)(2,1)S(1)} %collective-permute-done.13) | copy-start | bytes 3145732
  114.9 4.5 %copy-start.49 = (bf16[8,208,512]{2,1,0:T(8,128)(2,1)S(1)}, bf16[8,208,512]{2,1,0:T(8,128)(2,1)}, u32[]{:S(2)}) copy-start(bf16[8,208,512]{2,1,0:T(8,128)(2,1)} %get-tuple-element.171) | copy-start | bytes 5111812
  115.0 4.6 %copy-start.33 = (bf16[512,1280]{1,0:T(8,128)(2,1)S(1)}, bf16[512,1280]{1,0:T(8,128)(2,1)}, u32[]{:S(2)}) copy-start(bf16[512,1280]{1,0:T(8,128)(2,1)} %get-tuple-element.165) | copy-start | bytes 3932164
  118.9 18.2 %collective-permute-start.20 = (bf16[512,768]{1,0:T(8,128)(2,1)}, bf16[512,768]{1,0:T(8,128)(2,1)}, u32[]{:S(2)}, u32[]{:S(2)}) collective-permute-start(bf16[512,768]{1,0:T(8,128)(2,1)} %side_grads.1), channel_id=1, source_target_pairs={{0,1},{1,0},{2,3},{3,2},{4,5},{5,4},{6,7},{7,6},{8,9},{9,8},{10,11... | collective-permute-start | bytes 2359304 | tf_op jit(solution)/shard_map/ppermute | solution.py:766
  119.4 17.7 %collective-permute-start.21 = (bf16[8,208,512]{2,1,0:T(8,128)(2,1)S(1)}, bf16[8,208,512]{2,1,0:T(8,128)(2,1)}, u32[]{:S(2)}, u32[]{:S(2)}) collective-permute-start(bf16[8,208,512]{2,1,0:T(8,128)(2,1)S(1)} %copy-done.49), channel_id=1, source_target_pairs={{0,1},{1,0},{2,3},{3,2},{4,5},{5,4},{6,7},{7,6},{8,9},{9,8},{10,11... | collective-permute-start | bytes 5111816 | tf_op jit(solution)/shard_map/ppermute | solution.py:766
  119.9 17.2 %collective-permute-start.19 = (bf16[2,2,2,32,1280]{4,3,2,1,0:T(8,128)(2,1)S(1)}, bf16[2,2,2,32,1280]{4,3,2,1,0:T(8,128)(2,1)}, u32[]{:S(2)}, u32[]{:S(2)}) collective-permute-start(bf16[2,2,2,32,1280]{4,3,2,1,0:T(8,128)(2,1)S(1)} %constant_dynamic-slice_fusion.7), channel_id=1, source_target_pairs={{0,2},{2,0},{1,3},{3,1},{4,6},{6,4},{5,7},{7,5},{8,10},{10,8},{9,1... | collective-permute-start | bytes 1966088 | tf_op jit(solution)/shard_map/ppermute | solution.py:766
  121.6 14.3 %collective-permute-start.18 = (bf16[2,2,1,64,1024]{4,3,2,1,0:T(8,128)(2,1)S(1)}, bf16[2,2,1,64,1024]{4,3,2,1,0:T(8,128)(2,1)S(1)}, u32[]{:S(2)}, u32[]{:S(2)}) collective-permute-start(bf16[2,2,1,64,1024]{4,3,2,1,0:T(8,128)(2,1)S(1)} %constant_dynamic-slice_fusion.8), channel_id=1, source_target_pairs={{0,4},{4,0},{8,12},{12,8},{16,20},{20,16},{24,28},{28,24},{1,5},{5... | collective-permute-start | bytes 1572872 | tf_op jit(solution)/shard_map/ppermute | solution.py:766
  137.2 17.7 %collective-permute-start.24 = (bf16[8,208,512]{2,1,0:T(8,128)(2,1)}, bf16[8,208,512]{2,1,0:T(8,128)(2,1)}, u32[]{:S(2)}, u32[]{:S(2)}) collective-permute-start(bf16[8,208,512]{2,1,0:T(8,128)(2,1)} %get-tuple-element.177), channel_id=1, source_target_pairs={{0,1},{1,0},{2,3},{3,2},{4,5},{5,4},{6,7},{7,6},{8,9},{9,8},{10,11... | collective-permute-start | bytes 5111816 | tf_op jit(solution)/shard_map/ppermute | solution.py:766
  138.7 15.6 %collective-permute-start.23 = (bf16[2,2,1,32,1280]{4,3,2,1,0:T(8,128)(2,1)S(1)}, bf16[2,2,1,32,1280]{4,3,2,1,0:T(8,128)(2,1)S(1)}, u32[]{:S(2)}, u32[]{:S(2)}) collective-permute-start(bf16[2,2,1,32,1280]{4,3,2,1,0:T(8,128)(2,1)S(1)} %constant_dynamic-slice_fusion.5), channel_id=1, source_target_pairs={{0,4},{4,0},{8,12},{12,8},{16,20},{20,16},{24,28},{28,24},{1,5},{5... | collective-permute-start | bytes 983048 | tf_op jit(solution)/shard_map/ppermute | solution.py:766
  141.2 11.8 %collective-permute-start.22 = (bf16[2,1,1,64,1024]{4,3,2,1,0:T(8,128)(2,1)}, bf16[2,1,1,64,1024]{4,3,2,1,0:T(8,128)(2,1)}, u32[]{:S(2)}, u32[]{:S(2)}) collective-permute-start(bf16[2,1,1,64,1024]{4,3,2,1,0:T(8,128)(2,1)} %constant_dynamic-slice_fusion.6), channel_id=1, source_target_pairs={{0,8},{4,12},{8,0},{12,4},{16,24},{20,28},{24,16},{28,20},{1,9},{5... | collective-permute-start | bytes 786440 | tf_op jit(solution)/shard_map/ppermute | solution.py:766
  141.4 9.3 %copy-start.4 = (s32[2,1600,1]{2,1,0:T(8,128)S(1)}, s32[2,1600,1]{2,1,0:T(8,128)}, u32[]{:S(2)}) copy-start(s32[2,1600,1]{2,1,0:T(8,128)} %constant.104.clone.picks_ref) | copy-start | bytes 38404
  141.4 9.3 %copy-start.19 = (bf16[2,208,256]{2,1,0:T(8,128)(2,1)S(1)}, bf16[2,208,256]{2,1,0:T(8,128)(2,1)}, u32[]{:S(2)}) copy-start(bf16[2,208,256]{2,1,0:T(8,128)(2,1)} %get-tuple-element.178) | copy-start | bytes 638980
  149.3 18.1 %collective-permute-start.25 = (bf16[2,2,1,64,768]{4,3,2,1,0:T(8,128)(2,1)}, bf16[2,2,1,64,768]{4,3,2,1,0:T(8,128)(2,1)}, u32[]{:S(2)}, u32[]{:S(2)}) collective-permute-start(bf16[2,2,1,64,768]{4,3,2,1,0:T(8,128)(2,1)} %bitcast.74), channel_id=1, source_target_pairs={{0,4},{4,0},{8,12},{12,8},{16,20},{20,16},{24,28},{28,24},{1,5},{5... | collective-permute-start | bytes 1179656 | tf_op jit(solution)/shard_map/ppermute | solution.py:766
  150.7 4.1 %copy-start.28 = (bf16[2,2,2,32,1280]{4,3,2,1,0:T(8,128)(2,1)S(1)}, bf16[2,2,2,32,1280]{4,3,2,1,0:T(8,128)(2,1)}, u32[]{:S(2)}) copy-start(bf16[2,2,2,32,1280]{4,3,2,1,0:T(8,128)(2,1)} %copy-done.27) | copy-start | bytes 1966084
  150.8 7.1 %collective-permute-start.28 = (bf16[416,256]{1,0:T(8,128)(2,1)}, bf16[416,256]{1,0:T(8,128)(2,1)S(1)}, u32[]{:S(2)}, u32[]{:S(2)}) collective-permute-start(bf16[416,256]{1,0:T(8,128)(2,1)} %bitcast.78), channel_id=1, source_target_pairs={{0,1},{1,0},{2,3},{3,2},{4,5},{5,4},{6,7},{7,6},{8,9},{9,8},{10,11... | collective-permute-start | bytes 638984 | tf_op jit(solution)/shard_map/ppermute | solution.py:766
  153.0 3.8 %copy-start.30 = (bf16[2,2,1,64,1024]{4,3,2,1,0:T(8,128)(2,1)S(1)}, bf16[2,2,1,64,1024]{4,3,2,1,0:T(8,128)(2,1)}, u32[]{:S(2)}) copy-start(bf16[2,2,1,64,1024]{4,3,2,1,0:T(8,128)(2,1)} %copy-done.29) | copy-start | bytes 1572868
  153.0 14.5 %collective-permute-start.29 = (bf16[416,256]{1,0:T(8,128)(2,1)}, bf16[416,256]{1,0:T(8,128)(2,1)S(1)}, u32[]{:S(2)}, u32[]{:S(2)}) collective-permute-start(bf16[416,256]{1,0:T(8,128)(2,1)} %bitcast.25), channel_id=1, source_target_pairs={{0,2},{2,0},{1,3},{3,1},{4,6},{6,4},{5,7},{7,5},{8,10},{10,8},{9,1... | collective-permute-start | bytes 638984 | tf_op jit(solution)/shard_map/ppermute | solution.py:766
  154.3 13.1 %collective-permute-start.30 = (bf16[416,256]{1,0:T(8,128)(2,1)}, bf16[416,256]{1,0:T(8,128)(2,1)S(1)}, u32[]{:S(2)}, u32[]{:S(2)}) collective-permute-start(bf16[416,256]{1,0:T(8,128)(2,1)} %bitcast.26), channel_id=1, source_target_pairs={{0,3},{1,2},{2,1},{3,0},{4,7},{5,6},{6,5},{7,4},{8,11},{9,10},{10,... | collective-permute-start | bytes 638984 | tf_op jit(solution)/shard_map/ppermute | solution.py:978
  155.0 12.5 %collective-permute-start.26 = (bf16[2,1,1,32,1280]{4,3,2,1,0:T(8,128)(2,1)S(1)}, bf16[2,1,1,32,1280]{4,3,2,1,0:T(8,128)(2,1)S(1)}, u32[]{:S(2)}, u32[]{:S(2)}) collective-permute-start(bf16[2,1,1,32,1280]{4,3,2,1,0:T(8,128)(2,1)S(1)} %constant_dynamic-slice_fusion.4), channel_id=1, source_target_pairs={{0,8},{4,12},{8,0},{12,4},{16,24},{20,28},{24,16},{28,20},{1,9},{5... | collective-permute-start | bytes 491528 | tf_op jit(solution)/shard_map/ppermute | solution.py:766
  157.8 9.6 %collective-permute-start.27 = (bf16[1,1,1,64,1024]{4,3,2,1,0:T(8,128)(2,1)S(1)}, bf16[1,1,1,64,1024]{4,3,2,1,0:T(8,128)(2,1)S(1)}, u32[]{:S(2)}, u32[]{:S(2)}) collective-permute-start(bf16[1,1,1,64,1024]{4,3,2,1,0:T(8,128)(2,1)S(1)} %constant_dynamic-slice_fusion.3), channel_id=1, source_target_pairs={{0,16},{4,20},{8,24},{12,28},{16,0},{20,4},{24,8},{28,12},{1,17},{... | collective-permute-start | bytes 393224 | tf_op jit(solution)/shard_map/ppermute | solution.py:766
  158.9 9.2 %copy-start.39 = (bf16[4,64,768]{2,1,0:T(8,128)(2,1)S(1)}, bf16[4,64,768]{2,1,0:T(8,128)(2,1)}, u32[]{:S(2)}) copy-start(bf16[4,64,768]{2,1,0:T(8,128)(2,1)} %get-tuple-element.191) | copy-start | bytes 1179652
  167.6 14.6 %collective-permute-start.33 = (bf16[64,1024]{1,0:T(8,128)(2,1)S(1)}, bf16[64,1024]{1,0:T(8,128)(2,1)}, u32[]{:S(2)}, u32[]{:S(2)}) collective-permute-start(bf16[64,1024]{1,0:T(8,128)(2,1)S(1)} %fusion.4), channel_id=1, source_target_pairs={{0,2},{2,0},{1,3},{3,1},{4,6},{6,4},{5,7},{7,5},{8,10},{10,8},{9,1... | collective-permute-start | bytes 393224 | tf_op jit(solution)/shard_map/ppermute | solution.py:766
  169.3 12.9 %collective-permute-start.31 = (bf16[2,1,1,64,768]{4,3,2,1,0:T(8,128)(2,1)S(1)}, bf16[2,1,1,64,768]{4,3,2,1,0:T(8,128)(2,1)S(1)}, u32[]{:S(2)}, u32[]{:S(2)}) collective-permute-start(bf16[2,1,1,64,768]{4,3,2,1,0:T(8,128)(2,1)S(1)} %constant_dynamic-slice_fusion.2), channel_id=1, source_target_pairs={{0,8},{4,12},{8,0},{12,4},{16,24},{20,28},{24,16},{28,20},{1,9},{5... | collective-permute-start | bytes 589832 | tf_op jit(solution)/shard_map/ppermute | solution.py:766
  171.1 11.1 %collective-permute-start.32 = (bf16[1,1,1,32,1280]{4,3,2,1,0:T(8,128)(2,1)S(1)}, bf16[1,1,1,32,1280]{4,3,2,1,0:T(8,128)(2,1)S(1)}, u32[]{:S(2)}, u32[]{:S(2)}) collective-permute-start(bf16[1,1,1,32,1280]{4,3,2,1,0:T(8,128)(2,1)S(1)} %constant_dynamic-slice_fusion.1), channel_id=1, source_target_pairs={{0,16},{4,20},{8,24},{12,28},{16,0},{20,4},{24,8},{28,12},{1,17},{... | collective-permute-start | bytes 245768 | tf_op jit(solution)/shard_map/ppermute | solution.py:766
  182.2 9.4 %copy-start.20 = (bf16[2,208,256]{2,1,0:T(8,128)(2,1)S(1)}, bf16[2,208,256]{2,1,0:T(8,128)(2,1)}, u32[]{:S(2)}) copy-start(bf16[2,208,256]{2,1,0:T(8,128)(2,1)} %get-tuple-element.214) | copy-start | bytes 638980
  182.2 16.1 %collective-permute-start.42 = (bf16[1,1,1,32,1280]{4,3,2,1,0:T(8,128)(2,1)S(1)}, bf16[1,1,1,32,1280]{4,3,2,1,0:T(8,128)(2,1)S(1)}, u32[]{:S(2)}, u32[]{:S(2)}) collective-permute-start(bf16[1,1,1,32,1280]{4,3,2,1,0:T(8,128)(2,1)S(1)} %add_convert_fusion.10), channel_id=1, source_target_pairs={{0,2},{2,0},{1,3},{3,1},{4,6},{6,4},{5,7},{7,5},{8,10},{10,8},{9,1... | collective-permute-start | bytes 245768 | tf_op jit(solution)/shard_map/ppermute | solution.py:766
  183.2 1.5 collective-permute-start.34
  185.6 8.2 %collective-permute-start.35 = (bf16[96,256]{1,0:T(8,128)(2,1)S(1)}, bf16[96,256]{1,0:T(8,128)(2,1)S(1)}, u32[]{:S(2)}, u32[]{:S(2)}) collective-permute-start(bf16[96,256]{1,0:T(8,128)(2,1)S(1)} %add.160), channel_id=1, source_target_pairs={{0,2},{2,0},{4,6},{6,4},{8,10},{10,8},{12,14},{14,12},{16,18},{18,... | collective-permute-start | bytes 147464 | tf_op jit(solution)/shard_map/ppermute | solution.py:864
  186.8 7.0 %collective-permute-start.36 = (bf16[96,256]{1,0:T(8,128)(2,1)S(1)}, bf16[96,256]{1,0:T(8,128)(2,1)S(1)}, u32[]{:S(2)}, u32[]{:S(2)}) collective-permute-start(bf16[96,256]{1,0:T(8,128)(2,1)S(1)} %add.160), channel_id=1, source_target_pairs={{0,4},{2,6},{4,0},{6,2},{8,12},{10,14},{12,8},{14,10},{16,20},{18,... | collective-permute-start | bytes 147464 | tf_op jit(solution)/shard_map/ppermute | solution.py:864
  187.5 6.3 %collective-permute-start.37 = (bf16[96,256]{1,0:T(8,128)(2,1)S(1)}, bf16[96,256]{1,0:T(8,128)(2,1)S(1)}, u32[]{:S(2)}, u32[]{:S(2)}) collective-permute-start(bf16[96,256]{1,0:T(8,128)(2,1)S(1)} %add.160), channel_id=1, source_target_pairs={{0,6},{2,4},{4,2},{6,0},{8,14},{10,12},{12,10},{14,8},{16,22},{18,... | collective-permute-start | bytes 147464 | tf_op jit(solution)/shard_map/ppermute | solution.py:864
  189.2 9.2 %collective-permute-start.41 = (bf16[1,1,1,64,768]{4,3,2,1,0:T(8,128)(2,1)S(1)}, bf16[1,1,1,64,768]{4,3,2,1,0:T(8,128)(2,1)S(1)}, u32[]{:S(2)}, u32[]{:S(2)}) collective-permute-start(bf16[1,1,1,64,768]{4,3,2,1,0:T(8,128)(2,1)S(1)} %constant_dynamic-slice_fusion), channel_id=1, source_target_pairs={{0,16},{4,20},{8,24},{12,28},{16,0},{20,4},{24,8},{28,12},{1,17},{... | collective-permute-start | bytes 294920 | tf_op jit(solution)/shard_map/ppermute | solution.py:766
  193.8 8.2 %copy-start.42 = (bf16[96,256]{1,0:T(8,128)(2,1)}, bf16[96,256]{1,0:T(8,128)(2,1)S(1)}, u32[]{:S(2)}) copy-start(bf16[96,256]{1,0:T(8,128)(2,1)S(1)} %add_add_fusion.a_ref) | copy-start | bytes 147460
  193.8 8.1 %collective-permute-start.38 = (bf16[96,256]{1,0:T(8,128)(2,1)S(1)}, bf16[96,256]{1,0:T(8,128)(2,1)S(1)}, u32[]{:S(2)}, u32[]{:S(2)}) collective-permute-start(bf16[96,256]{1,0:T(8,128)(2,1)S(1)} %add_add_fusion.a_ref), channel_id=1, source_target_pairs={{0,8},{2,10},{4,12},{6,14},{8,0},{10,2},{12,4},{14,6},{16,24},{18,... | collective-permute-start | bytes 147464 | tf_op jit(solution)/shard_map/ppermute | solution.py:864
  194.2 7.8 %collective-permute-start.39 = (bf16[96,256]{1,0:T(8,128)(2,1)S(1)}, bf16[96,256]{1,0:T(8,128)(2,1)S(1)}, u32[]{:S(2)}, u32[]{:S(2)}) collective-permute-start(bf16[96,256]{1,0:T(8,128)(2,1)S(1)} %add_add_fusion.a_ref), channel_id=1, source_target_pairs={{0,16},{2,18},{4,20},{6,22},{8,24},{10,26},{12,28},{14,30},{16,0},... | collective-permute-start | bytes 147464 | tf_op jit(solution)/shard_map/ppermute | solution.py:864
  196.1 5.9 %collective-permute-start.40 = (bf16[96,256]{1,0:T(8,128)(2,1)S(1)}, bf16[96,256]{1,0:T(8,128)(2,1)S(1)}, u32[]{:S(2)}, u32[]{:S(2)}) collective-permute-start(bf16[96,256]{1,0:T(8,128)(2,1)S(1)} %add_add_fusion.a_ref), channel_id=1, source_target_pairs={{0,24},{2,26},{4,28},{6,30},{8,16},{10,18},{12,20},{14,22},{16,8},... | collective-permute-start | bytes 147464 | tf_op jit(solution)/shard_map/ppermute | solution.py:864
  200.0 6.3 %copy-start.1 = (s32[4,392]{1,0:T(4,128)S(1)}, s32[4,392]{1,0:T(4,128)}, u32[]{:S(2)}) copy-start(s32[4,392]{1,0:T(4,128)} %param.36) | copy-start | bytes 18820
  200.8 4.7 %collective-permute-start.43 = (bf16[64,768]{1,0:T(8,128)(2,1)S(1)}, bf16[64,768]{1,0:T(8,128)(2,1)S(1)}, u32[]{:S(2)}, u32[]{:S(2)}) collective-permute-start(bf16[64,768]{1,0:T(8,128)(2,1)S(1)} %fusion.5), channel_id=1, source_target_pairs={{0,2},{2,0},{1,3},{3,1},{4,6},{6,4},{5,7},{7,5},{8,10},{10,8},{9,1... | collective-permute-start | bytes 294920 | tf_op jit(solution)/shard_map/ppermute | solution.py:766
  (30 other events, 47.5 us)
